TPU v7x, 32 devices: a whole 2x2x4 slice. The times are simulated.
32 devices in a mesh: dp: 4 (over x, core), context: 4 (over z), tensor: 2 (over y).
Axes of the slice: x: 2, y: 2, z: 4, core: 2. Of those that a mesh axis runs over, the one named last changes fastest.
Arguments:
- tokens: bfloat16 [4, 4096, 768], P('dp', 'context'), may hold values from -6 to 6
- positions: int32 [4, 4096], P('dp', 'context'), may hold values from 0 to 4095, each once within a row
- first_gain: float32 [768], replicated, may hold values from 0.5 to 1.5
- first_shift: float32 [768], replicated, may hold values from -3 to 3
- second_gain: float32 [768], replicated, may hold values from 0.5 to 1.5
- second_shift: float32 [768], replicated, may hold values from -3 to 3
- w_query: bfloat16 [768, 768], P('dp', 'tensor'), may hold values from -0.21875 to 0.21875
- w_key: bfloat16 [768, 768], P('dp', 'tensor'), may hold values from -0.21875 to 0.21875
- w_value: bfloat16 [768, 768], P('dp', 'tensor'), may hold values from -0.21875 to 0.21875
- query_bias: float32 [768], P('tensor'), may hold values from -3 to 3
- key_bias: float32 [768], P('tensor'), may hold values from -3 to 3
- value_bias: float32 [768], P('tensor'), may hold values from -3 to 3
- w_out: bfloat16 [768, 768], P('tensor', 'dp'), may hold values from -0.875 to 0.875
- out_bias: float32 [768], replicated, may hold values from -3 to 3
- w_up: bfloat16 [768, 3072], P('dp', 'tensor'), may hold values from -0.21875 to 0.21875
- up_bias: float32 [3072], P('tensor'), may hold values from -3 to 3
- w_down: bfloat16 [3072, 768], P('tensor', 'dp'), may hold values from -0.109375 to 0.109375
- down_bias: float32 [768], replicated, may hold values from -3 to 3
- cotangent: bfloat16 [4, 4096, 768], P('dp', 'context'), may hold values from -6 to 6
Outputs:
- block_out: bfloat16 [4, 4096, 768], P('dp', 'context')
- grad_tokens: float32 [4, 4096, 768], P('dp', 'context')
- grad_first_gain: float32 [768], replicated
- grad_first_shift: float32 [768], replicated
- grad_second_gain: float32 [768], replicated
- grad_second_shift: float32 [768], replicated
- grad_w_query: float32 [768, 768], P('dp', 'tensor')
- grad_w_key: float32 [768, 768], P('dp', 'tensor')
- grad_w_value: float32 [768, 768], P('dp', 'tensor')
- grad_query_bias: float32 [768], P('tensor')
- grad_key_bias: float32 [768], P('tensor')
- grad_value_bias: float32 [768], P('tensor')
- grad_w_out: float32 [768, 768], P('tensor', 'dp')
- grad_out_bias: float32 [768], replicated
- grad_w_up: float32 [768, 3072], P('dp', 'tensor')
- grad_up_bias: float32 [3072], P('tensor')
- grad_w_down: float32 [3072, 768], P('tensor', 'dp')
- grad_down_bias: float32 [768], replicated
Inputs may be any that keep to these rules, and one draw needn't show every extreme that they name: Each row of positions holds every position 0 to 4095 exactly once.
All inputs are finite; a program needn't handle non-finite values.
Results may differ from a plain program's by a relative error of at most 0.014.
Values may be sent and summed in bfloat16 or wider, within the bound.
A program may use at most 256 MiB of HBM per device.

v0:
```python
import math

import jax
import jax.numpy as jnp
from jax import lax
from jax.sharding import PartitionSpec as P

HEAD_DIM = 64
ROT_DIM = 16


epsilon = 1e-05


def rotary_tables(places):
    frequency = jnp.exp(
        jnp.arange(ROT_DIM // 2, dtype=jnp.float32) * (-2.0 * math.log(10000.0) / ROT_DIM)
    )
    angle_rad = places.astype(jnp.float32)[..., None] * frequency
    return (jnp.cos(angle_rad), jnp.sin(angle_rad))


def rotate_heads(field, cosine, sine):
    half_rot = ROT_DIM // 2
    leading = field[..., :half_rot]
    trailing = field[..., half_rot:ROT_DIM]
    return jnp.concatenate(
        [
            leading * cosine - trailing * sine,
            trailing * cosine + leading * sine,
            field[..., ROT_DIM:],
        ],
        axis=-1,
    )


def normalize(values):
    row_mean = jnp.mean(values, axis=-1, keepdims=True)
    centred = values - row_mean
    row_var = jnp.mean(centred * centred, axis=-1, keepdims=True)
    inv_std = lax.rsqrt(row_var + epsilon)
    return (centred * inv_std, inv_std)


def norm_back(upstream, plain, inv_std, gain):
    tilted = upstream * gain
    first_mean = jnp.mean(tilted, axis=-1, keepdims=True)
    second_mean = jnp.mean(tilted * plain, axis=-1, keepdims=True)
    input_term = inv_std * (tilted - first_mean - plain * second_mean)
    return (input_term, jnp.sum(upstream * plain, axis=0), jnp.sum(upstream, axis=0))


def to_items(field, seq_count, length, head_count):
    return (
        field.reshape(seq_count, length, head_count, HEAD_DIM)
        .transpose(2, 0, 1, 3)
        .reshape(head_count * seq_count, length, HEAD_DIM)
    )


def from_items(items, seq_count, length, head_count):
    return (
        items.reshape(head_count, seq_count, length, HEAD_DIM)
        .transpose(1, 2, 0, 3)
        .reshape(seq_count, length, head_count * HEAD_DIM)
    )


def place_items(places, head_count):
    return jnp.broadcast_to(places[None], (head_count,) + places.shape).reshape(
        head_count * places.shape[0], places.shape[1]
    )


def item_scores(query_item, key_item, query_places, key_places):
    scores = jnp.einsum(
        "qd,kd->qk", query_item, key_item, preferred_element_type=jnp.float32
    ) * HEAD_DIM ** (-0.5)
    allowed = key_places[None, :] <= query_places[:, None]
    return (jnp.where(allowed, scores, -1e30), allowed)


def item_probs(query_item, key_item, log_total, query_places, key_places):
    scores, allowed = item_scores(query_item, key_item, query_places, key_places)
    return jnp.where(allowed, jnp.exp(scores - log_total[:, None]), 0.0)


def attend_item(query_item, key_item, value_item, query_places, key_places):
    scores, allowed = item_scores(query_item, key_item, query_places, key_places)
    row_max = jnp.max(scores, axis=-1, keepdims=True)
    exp_scores = jnp.exp(scores - row_max)
    row_total = jnp.sum(exp_scores, axis=-1, keepdims=True)
    probs_low = (exp_scores / row_total).astype(jnp.bfloat16)
    mixed_item = jnp.einsum("qk,kd->qd", probs_low, value_item, preferred_element_type=jnp.float32)
    return (mixed_item, row_max[:, 0] + jnp.log(row_total[:, 0]))


def attend_back(query_item, key_item, value_item, log_total, grad_item, query_places, key_places):
    probs = item_probs(query_item, key_item, log_total, query_places, key_places)
    probs_low = probs.astype(jnp.bfloat16)
    grad_value = jnp.einsum("qk,qd->kd", probs_low, grad_item, preferred_element_type=jnp.float32)
    grad_probs = jnp.einsum("qd,kd->qk", grad_item, value_item, preferred_element_type=jnp.float32)
    row_delta = jnp.sum(probs * grad_probs, axis=-1, keepdims=True)
    grad_scores = (probs * (grad_probs - row_delta)).astype(jnp.bfloat16)
    grad_query = jnp.einsum(
        "qk,kd->qd", grad_scores, key_item, preferred_element_type=jnp.float32
    ) * HEAD_DIM ** (-0.5)
    grad_key = jnp.einsum(
        "qk,qd->kd", grad_scores, query_item, preferred_element_type=jnp.float32
    ) * HEAD_DIM ** (-0.5)
    return (grad_query, grad_key, grad_value)


def body(
    tokens,
    positions,
    first_gain,
    first_shift,
    second_gain,
    second_shift,
    w_query,
    w_key,
    w_value,
    query_bias,
    key_bias,
    value_bias,
    w_out,
    out_bias,
    w_up,
    up_bias,
    w_down,
    down_bias,
    cotangent,
):
    seq_count, block_len, model_width = tokens.shape
    row_count = seq_count * block_len
    flat_in = tokens.reshape(row_count, model_width).astype(jnp.float32)
    upstream = cotangent.reshape(row_count, model_width)
    full_query, full_key, full_value, full_up = (
        lax.all_gather(w_query, "dp", axis=0, tiled=True),
        lax.all_gather(w_key, "dp", axis=0, tiled=True),
        lax.all_gather(w_value, "dp", axis=0, tiled=True),
        lax.all_gather(w_up, "dp", axis=0, tiled=True),
    )
    full_out, full_down = (
        lax.all_gather(w_out, "dp", axis=1, tiled=True),
        lax.all_gather(w_down, "dp", axis=1, tiled=True),
    )
    part_width = full_query.shape[1]
    head_count = part_width // HEAD_DIM
    half_rot = ROT_DIM // 2
    plain_one, inv_one = normalize(flat_in)
    plain_two, inv_two = (plain_one, inv_one)
    normed_one = (plain_one * first_gain + first_shift).astype(jnp.bfloat16)
    normed_two = (plain_two * second_gain + second_shift).astype(jnp.bfloat16)
    cosine, sine = rotary_tables(positions)
    cosine = cosine.reshape(row_count, 1, half_rot)
    sine = sine.reshape(row_count, 1, half_rot)

    def project(weight, bias):
        return jnp.dot(normed_one, weight, preferred_element_type=jnp.float32) + bias

    query_rot = rotate_heads(
        project(full_query, query_bias).reshape(row_count, head_count, HEAD_DIM), cosine, sine
    ).astype(jnp.bfloat16)
    key_rot = rotate_heads(
        project(full_key, key_bias).reshape(row_count, head_count, HEAD_DIM), cosine, sine
    ).astype(jnp.bfloat16)
    value_low = project(full_value, value_bias).astype(jnp.bfloat16)
    key_all, value_all, key_places = (
        lax.all_gather(
            key_rot.reshape(seq_count, block_len, part_width), "context", axis=1, tiled=True
        ),
        lax.all_gather(
            value_low.reshape(seq_count, block_len, part_width), "context", axis=1, tiled=True
        ),
        lax.all_gather(positions, "context", axis=1, tiled=True),
    )
    total_len = key_all.shape[1]
    query_items = to_items(query_rot, seq_count, block_len, head_count)
    key_items = to_items(key_all, seq_count, total_len, head_count)
    value_items = to_items(value_all, seq_count, total_len, head_count)
    own_place_items = place_items(positions, head_count)
    all_place_items = place_items(key_places, head_count)

    def forward_item(pieces):
        return attend_item(pieces[0], pieces[1], pieces[2], pieces[3], pieces[4])

    mixed_items, log_totals = lax.map(
        forward_item, (query_items, key_items, value_items, own_place_items, all_place_items)
    )
    mixed_out = (
        from_items(mixed_items, seq_count, block_len, head_count)
        .reshape(row_count, part_width)
        .astype(jnp.bfloat16)
    )
    inner_pre = jnp.dot(normed_two, full_up, preferred_element_type=jnp.float32) + up_bias
    hidden = jax.nn.gelu(inner_pre, approximate=False).astype(jnp.bfloat16)
    partial_out = jnp.dot(mixed_out, full_out, preferred_element_type=jnp.float32) + jnp.dot(
        hidden, full_down, preferred_element_type=jnp.float32
    )
    summed = lax.psum(partial_out, "tensor")
    block_out = (
        (flat_in + summed + out_bias + down_bias)
        .astype(jnp.bfloat16)
        .reshape(seq_count, block_len, model_width)
    )
    grad_wo = jnp.dot(mixed_out.T, upstream, preferred_element_type=jnp.float32)
    grad_wd = jnp.dot(hidden.T, upstream, preferred_element_type=jnp.float32)
    grad_out_sum = jnp.sum(upstream.astype(jnp.float32), axis=0)
    grad_mixed = jnp.dot(upstream, full_out.T, preferred_element_type=jnp.float32).astype(
        jnp.bfloat16
    )
    grad_hidden = jnp.dot(upstream, full_down.T, preferred_element_type=jnp.float32)
    unused_out, gelu_back = jax.vjp(
        lambda inputs: jax.nn.gelu(inputs, approximate=False), inner_pre
    )
    grad_inner = gelu_back(grad_hidden)[0].astype(jnp.bfloat16)
    grad_ub = jnp.sum(grad_inner.astype(jnp.float32), axis=0)
    grad_wu = jnp.dot(normed_two.T, grad_inner, preferred_element_type=jnp.float32)
    back_two = jnp.dot(grad_inner, full_up.T, preferred_element_type=jnp.float32)
    grad_items = to_items(grad_mixed, seq_count, block_len, head_count)

    def backward_item(pieces):
        return attend_back(
            pieces[0], pieces[1], pieces[2], pieces[3], pieces[4], pieces[5], pieces[6]
        )

    grad_query_items, grad_key_items, grad_value_items = lax.map(
        backward_item,
        (
            query_items,
            key_items,
            value_items,
            log_totals,
            grad_items,
            own_place_items,
            all_place_items,
        ),
    )
    grad_key_all = from_items(grad_key_items, seq_count, total_len, head_count)
    grad_value_all = from_items(grad_value_items, seq_count, total_len, head_count)
    key_sum, value_sum = (
        lax.psum_scatter(grad_key_all, "context", scatter_dimension=1, tiled=True),
        lax.psum_scatter(grad_value_all, "context", scatter_dimension=1, tiled=True),
    )
    grad_query_rot = from_items(grad_query_items, seq_count, block_len, head_count).reshape(
        row_count, head_count, HEAD_DIM
    )
    grad_query_pre = (
        rotate_heads(grad_query_rot, cosine, -sine)
        .reshape(row_count, part_width)
        .astype(jnp.bfloat16)
    )
    grad_key_pre = (
        rotate_heads(key_sum.reshape(row_count, head_count, HEAD_DIM), cosine, -sine)
        .reshape(row_count, part_width)
        .astype(jnp.bfloat16)
    )
    grad_value_pre = value_sum.reshape(row_count, part_width).astype(jnp.bfloat16)
    grad_qb = jnp.sum(grad_query_pre.astype(jnp.float32), axis=0)
    grad_kb = jnp.sum(grad_key_pre.astype(jnp.float32), axis=0)
    grad_vb = jnp.sum(grad_value_pre.astype(jnp.float32), axis=0)
    grad_wq = jnp.dot(normed_one.T, grad_query_pre, preferred_element_type=jnp.float32)
    grad_wk = jnp.dot(normed_one.T, grad_key_pre, preferred_element_type=jnp.float32)
    grad_wv = jnp.dot(normed_one.T, grad_value_pre, preferred_element_type=jnp.float32)
    back_one = (
        jnp.dot(grad_query_pre, full_query.T, preferred_element_type=jnp.float32)
        + jnp.dot(grad_key_pre, full_key.T, preferred_element_type=jnp.float32)
        + jnp.dot(grad_value_pre, full_value.T, preferred_element_type=jnp.float32)
    )
    total_one, total_two = (
        lax.psum(back_one.astype(jnp.bfloat16), "tensor").astype(jnp.float32),
        lax.psum(back_two.astype(jnp.bfloat16), "tensor").astype(jnp.float32),
    )
    input_one, grad_g1, grad_s1 = norm_back(total_one, plain_one, inv_one, first_gain)
    input_two, grad_g2, grad_s2 = norm_back(total_two, plain_two, inv_two, second_gain)
    grad_tokens = (upstream.astype(jnp.float32) + input_one + input_two).reshape(
        seq_count, block_len, model_width
    )
    sum_g1, sum_s1, sum_g2, sum_s2, sum_qb, sum_kb, sum_vb, sum_ub, sum_ob = lax.psum(
        (grad_g1, grad_s1, grad_g2, grad_s2, grad_qb, grad_kb, grad_vb, grad_ub, grad_out_sum),
        ("dp", "context"),
    )
    whole_q, whole_k, whole_v, whole_u, whole_o, whole_d = (
        lax.psum(grad_wq.astype(jnp.bfloat16), "context").astype(jnp.float32),
        lax.psum(grad_wk.astype(jnp.bfloat16), "context").astype(jnp.float32),
        lax.psum(grad_wv.astype(jnp.bfloat16), "context").astype(jnp.float32),
        lax.psum(grad_wu.astype(jnp.bfloat16), "context").astype(jnp.float32),
        lax.psum(grad_wo.astype(jnp.bfloat16), "context").astype(jnp.float32),
        lax.psum(grad_wd.astype(jnp.bfloat16), "context").astype(jnp.float32),
    )
    shard_query, shard_key, shard_value, shard_up = (
        lax.psum_scatter(
            whole_q.astype(jnp.bfloat16), "dp", scatter_dimension=0, tiled=True
        ).astype(jnp.float32),
        lax.psum_scatter(
            whole_k.astype(jnp.bfloat16), "dp", scatter_dimension=0, tiled=True
        ).astype(jnp.float32),
        lax.psum_scatter(
            whole_v.astype(jnp.bfloat16), "dp", scatter_dimension=0, tiled=True
        ).astype(jnp.float32),
        lax.psum_scatter(
            whole_u.astype(jnp.bfloat16), "dp", scatter_dimension=0, tiled=True
        ).astype(jnp.float32),
    )
    shard_out, shard_down = (
        lax.psum_scatter(
            whole_o.astype(jnp.bfloat16), "dp", scatter_dimension=1, tiled=True
        ).astype(jnp.float32),
        lax.psum_scatter(
            whole_d.astype(jnp.bfloat16), "dp", scatter_dimension=1, tiled=True
        ).astype(jnp.float32),
    )
    return (
        block_out,
        grad_tokens,
        sum_g1,
        sum_s1,
        sum_g2,
        sum_s2,
        shard_query,
        shard_key,
        shard_value,
        sum_qb,
        sum_kb,
        sum_vb,
        shard_out,
        sum_ob,
        shard_up,
        sum_ub,
        shard_down,
        sum_ob,
    )


def solution(mesh):
    return jax.shard_map(
        body,
        mesh=mesh,
        in_specs=(
            P("dp", "context", None),
            P("dp", "context"),
            P(),
            P(),
            P(),
            P(),
            P("dp", "tensor"),
            P("dp", "tensor"),
            P("dp", "tensor"),
            P("tensor"),
            P("tensor"),
            P("tensor"),
            P("tensor", "dp"),
            P(),
            P("dp", "tensor"),
            P("tensor"),
            P("tensor", "dp"),
            P(),
            P("dp", "context", None),
        ),
        out_specs=(
            P("dp", "context", None),
            P("dp", "context", None),
            P(),
            P(),
            P(),
            P(),
            P("dp", "tensor"),
            P("dp", "tensor"),
            P("dp", "tensor"),
            P("tensor"),
            P("tensor"),
            P("tensor"),
            P("tensor", "dp"),
            P(),
            P("dp", "tensor"),
            P("tensor"),
            P("tensor", "dp"),
            P(),
        ),
        check_vma=False,
    )
```

profile of v0, /device:TPU:0, one launch (start us, length us, event | category | flops | bytes accessed | tf_op | source)
XLA Modules:
  0.0 1243.1 jit_solution(3358784750447216275)
XLA Ops:
  11.2 9.0 all_gather.28
  20.2 7.6 all_gather.29
  32.6 7.6 all_gather.31
  45.8 13.6 %all_gather.27 = s32[1,4096]{1,0:T(1,128)S(1)} all-gather(s32[1,1024]{1,0:T(1,128)S(1)} %copy-done.39), channel_id=1, replica_groups=mesh['dp'=4,'context'=4,'tensor'=2] {'context'}, dimensions={1}, use_global_device_ids=true | all-gather | bytes 20480 | tf_op jit(solution)/shard_map/all_gather | solution.py:177
  61.9 7.6 all_gather.33
  72.8 24.4 %all-gather.6.cloned.1.call-done = bf16[1,4096,384]{1,2,0:T(8,128)(2,1)} async-done(((bf16[1,1024,384]{1,2,0:T(8,128)(2,1)}), bf16[1,4096,384]{1,2,0:T(8,128)(2,1)}) %all-gather.6.cloned.1.call-update) | async-done | bytes 3145744 | tf_op jit(solution)/shard_map/all_gather | solution.py:171
  97.2 6.6 copy.43
  103.8 57.2 %all-gather.12.cloned.1.call-done = bf16[4096,384]{1,0:T(8,128)(2,1)} async-done(((bf16[1024,384]{1,0:T(8,128)(2,1)}), bf16[4096,384]{1,0:T(8,128)(2,1)}) %all-gather.12.cloned.1.call-update) | async-done | bytes 3145744 | tf_op jit(solution)/shard_map/all_gather | solution.py:174
  164.2 4.6 copy.44
  168.8 116.1 %while.28 = (s32[]{:T(128)}, bf16[6,1024,64]{1,2,0:T(8,128)(2,1)}, f32[6,1024]{1,0:T(8,128)S(1)}, s32[6,4096]{1,0:T(8,128)S(1)}, s32[6,1024]{1,0:T(8,128)S(1)}, ...) while((s32[]{:T(128)}, bf16[6,1024,64]{1,2,0:T(8,128)(2,1)}, ...), condition=%wide.region_5.6_spmd.clone, body=%wide.region_2.5_spmd.sunk.clone | while | flops 1136655360 | bytes 120207480 | solution.py:189
  173.1 4.7 fusion.188
  178.9 9.3 fusion.189
  192.3 4.7 fusion.188
  198.6 9.3 fusion.189
  212.1 4.7 fusion.188
  217.9 9.3 fusion.189
  231.4 4.7 fusion.188
  237.2 9.3 fusion.189
  250.6 4.7 fusion.188
  256.4 9.3 fusion.189
  269.8 4.7 fusion.188
  275.6 9.3 fusion.189
  284.9 232.6 %while.29 = (s32[]{:T(128)}, f32[6,1024,64]{1,2,0:T(8,128)}, f32[6,4096,64]{1,2,0:T(8,128)}, f32[6,4096,64]{1,2,0:T(8,128)}, s32[6,4096]{1,0:T(8,128)S(1)}, /*in...) while((s32[]{:T(128)}, f32[6,1024,64]{1,2,0:T(8,128)}, ...), condition=%wide.region_9.10_spmd.clone, body=%wide.region_7.9_spmd.sunk.clone | while | flops 2730818560 | bytes 132469880 | solution.py:229
  285.1 9.4 fusion.198
  294.5 9.7 multiply_reduce_fusion.3
  304.2 7.9 multiply_convert_fusion.4
  315.7 4.6 fusion.199
  323.9 9.4 fusion.198
  333.3 9.7 multiply_reduce_fusion.3
  342.9 7.9 multiply_convert_fusion.4
  354.4 4.6 fusion.199
  362.6 9.4 fusion.198
  372.0 9.7 multiply_reduce_fusion.3
  381.7 7.9 multiply_convert_fusion.4
  393.2 4.6 fusion.199
  401.3 9.4 fusion.198
  410.8 9.6 multiply_reduce_fusion.3
  420.4 7.9 multiply_convert_fusion.4
  431.9 4.6 fusion.199
  440.0 9.4 fusion.198
  449.5 9.7 multiply_reduce_fusion.3
  459.1 7.9 multiply_convert_fusion.4
  478.8 9.4 fusion.198
  488.2 9.6 multiply_reduce_fusion.3
  497.8 7.9 multiply_convert_fusion.4
  509.3 4.6 fusion.199
  519.0 20.0 %multiply_convert_fusion.1 = (bf16[1024,1536]{1,0:T(8,128)(2,1)}, f32[1024,1536]{1,0:T(8,128)}, f32[1024,1536]{1,0:T(8,128)}) fusion(f32[1536]{0:T(1024)S(1)} %copy-done.46, bf16[768,1536]{1,0:T(8,128)(2,1)} %all-gather.8.cloned.1.call-done, bf16[1,1024,768]{2,1,0:T(8,128)(2,1)S(1)} %copy-done.2, f32[768]{0:T(1024)S(1)} %copy-done.47, ...), kind=kOutput, calls=%fused_computation.65 | convolution fusion | flops 2524446720 | bytes 19681280 | tf_op jit(solution)/shard_map/dot_general | solution.py:197
  541.0 10.3 convert_reduce_fusion
  557.3 5.8 convolution_convert_fusion
  566.9 60.3 %reduce-scatter.9.cloned.1.call-done = f32[1,1024,384]{1,2,0:T(8,128)} async-done(((f32[1,4096,384]{1,2,0:T(8,128)}), f32[1,1024,384]{1,2,0:T(8,128)}) %reduce-scatter.9.cloned.1.call-update) | async-done | bytes 1572880 | tf_op jit(solution)/shard_map/reduce_scatter | solution.py:244
  636.4 104.2 %reduce-scatter.11.cloned.1.call-done = f32[1,1024,384]{1,2,0:T(8,128)} async-done(((f32[1,4096,384]{1,2,0:T(8,128)}), f32[1,1024,384]{1,2,0:T(8,128)}) %reduce-scatter.11.cloned.1.call-update) | async-done | bytes 1572880 | tf_op jit(solution)/shard_map/reduce_scatter | solution.py:245
  744.4 21.3 %reduce-scatter.19.cloned.1.call-done = bf16[384,192]{0,1:T(8,128)(2,1)} async-done(((bf16[384,768]{0,1:T(8,128)(2,1)}), bf16[384,192]{0,1:T(8,128)(2,1)}) %reduce-scatter.19.cloned.1.call-update) | async-done | bytes 147472 | tf_op jit(solution)/shard_map/reduce_scatter | solution.py:308
  765.7 35.6 %reduce-scatter.21.cloned.1.call-done = bf16[192,1536]{1,0:T(8,128)(2,1)} async-done(((bf16[768,1536]{1,0:T(8,128)(2,1)}), bf16[192,1536]{1,0:T(8,128)(2,1)}) %reduce-scatter.21.cloned.1.call-update) | async-done | bytes 589840 | tf_op jit(solution)/shard_map/reduce_scatter | solution.py:303
  801.4 35.8 %reduce-scatter.23.cloned.1.call-done = bf16[1536,192]{0,1:T(8,128)(2,1)} async-done(((bf16[1536,768]{0,1:T(8,128)(2,1)}), bf16[1536,192]{0,1:T(8,128)(2,1)}) %reduce-scatter.23.cloned.1.call-update) | async-done | bytes 589840 | tf_op jit(solution)/shard_map/reduce_scatter | solution.py:311
  837.2 25.0 %reduce-scatter.13.cloned.1.call-done = bf16[192,384]{1,0:T(8,128)(2,1)} async-done(((bf16[768,384]{1,0:T(8,128)(2,1)}), bf16[192,384]{1,0:T(8,128)(2,1)}) %reduce-scatter.13.cloned.1.call-update) | async-done | bytes 147472 | tf_op jit(solution)/shard_map/reduce_scatter | solution.py:294
  862.2 24.6 %reduce-scatter.15.cloned.1.call-done = bf16[192,384]{1,0:T(8,128)(2,1)} async-done(((bf16[768,384]{1,0:T(8,128)(2,1)}), bf16[192,384]{1,0:T(8,128)(2,1)}) %reduce-scatter.15.cloned.1.call-update) | async-done | bytes 147472 | tf_op jit(solution)/shard_map/reduce_scatter | solution.py:297
  886.8 24.5 %reduce-scatter.17.cloned.1.call-done = bf16[192,384]{1,0:T(8,128)(2,1)} async-done(((bf16[768,384]{1,0:T(8,128)(2,1)}), bf16[192,384]{1,0:T(8,128)(2,1)}) %reduce-scatter.17.cloned.1.call-update) | async-done | bytes 147472 | tf_op jit(solution)/shard_map/reduce_scatter | solution.py:300
  911.4 6.4 convolution_convert_fusion.2
  923.3 5.3 fusion.121
  931.7 59.9 %all-reduce.9.cloned.1.call-done = (bf16[192,384]{1,0:T(8,128)(2,1)}, bf16[192,384]{1,0:T(8,128)(2,1)}, bf16[192,384]{1,0:T(8,128)(2,1)}, bf16[384,192]{0,1:T(8,...) async-done(((bf16[192,384]{1,0:T(8,128)(2,1)}, bf16[192,384]{1,0:T(8,128)(2,1)}, bf16[192,384]{1,0:T(8,128)(2,1)}, bf16[384,192]{0,1:T(8,128)(2,1)}, ...) | async-done | bytes 1769488 | tf_op jit(solution)/shard_map/psum | solution.py:286
  999.0 80.3 %all-reduce.11.cloned.1.call-done = (bf16[1024,768]{1,0:T(8,128)(2,1)}, bf16[1024,768]{1,0:T(8,128)(2,1)}) async-done(((bf16[1024,768]{1,0:T(8,128)(2,1)}, bf16[1024,768]{1,0:T(8,128)(2,1)}), (bf16[1024,768]{1,0:T(8,128)(2,1)}, bf16[1024,768]{1,0:T(8,128)(2,1)})) %all-reduce.11.cloned.1.call-update) | async-done | bytes 3145744 | tf_op jit(solution)/shard_map/psum | solution.py:274
  1083.7 84.1 %all-reduce.7.cloned.1.call-done = f32[1024,768]{1,0:T(8,128)} async-done(((f32[1024,768]{1,0:T(8,128)}), f32[1024,768]{1,0:T(8,128)}) %all-reduce.7.cloned.1.call-update) | async-done | bytes 3145744 | tf_op jit(solution)/shard_map/psum | solution.py:202
  1167.9 5.9 convert_reduce_fusion.4
  1173.7 62.1 %all-reduce = (f32[768]{0:T(1024)}, f32[768]{0:T(1024)}, f32[768]{0:T(1024)}, f32[768]{0:T(1024)}, f32[384]{0:T(512)}, /*index=5*/f32[384]{0:T(512)}, f32[384]{0:T(512)}, f32[768]{0:T(1024)S(1)}, f32[1536]{0:T(1024)}) all-reduce(f32[768]{0:T(1024)S(1)} %get-tuple-element.168, ...), channel_id=1, replica_groups=mesh['dp'=4,'context'=4,'tensor'=2] {'dp','context'}, use_global_device_ids=true, to_apply=%region_19.20 | all-reduce | flops 6528 | bytes 52224 | tf_op jit(solution)/shard_map/psum | solution.py:281
  (263 shorter events, 149.6 us)
Async XLA Ops:
  7.2 20.6 %copy-start.1 = (bf16[1,1024,768]{2,1,0:T(8,128)(2,1)S(1)}, bf16[1,1024,768]{2,1,0:T(8,128)(2,1)}, u32[]{:S(2)}) copy-start(bf16[1,1024,768]{2,1,0:T(8,128)(2,1)} %param.23) | copy-start | bytes 4718596
  7.2 4.0 copy-start.30
  7.2 13.0 %copy-start.31 = (bf16[192,384]{1,0:T(8,128)(2,1)S(1)}, bf16[192,384]{1,0:T(8,128)(2,1)}, u32[]{:S(2)}) copy-start(bf16[192,384]{1,0:T(8,128)(2,1)} %param.30) | copy-start | bytes 442372
  7.2 20.6 %copy-start.39 = (s32[1,1024]{1,0:T(1,128)S(1)}, s32[1,1024]{1,0:T(1,128)}, u32[]{:S(2)}) copy-start(s32[1,1024]{1,0:T(1,128)} %param.24) | copy-start | bytes 12292
  7.2 20.6 %copy-start.37 = (f32[768]{0:T(1024)S(1)}, f32[768]{0:T(1024)}, u32[]{:S(2)}) copy-start(f32[768]{0:T(1024)} %param.25) | copy-start | bytes 9220
  7.2 20.6 %copy-start.40 = (f32[768]{0:T(1024)S(1)}, f32[768]{0:T(1024)}, u32[]{:S(2)}) copy-start(f32[768]{0:T(1024)} %param.26) | copy-start | bytes 9220
  7.3 89.9 %all-gather.6.cloned.1.call-start = ((), (), s32[]{:S(2)}) async-start(), calls=%async_computation.8 | async-start | bytes 3932160 | tf_op jit(solution)/shard_map/all_gather | solution.py:171
  9.1 19.4 %copy-start.48 = (f32[384]{0:T(512)S(1)}, f32[384]{0:T(512)}, u32[]{:S(2)}) copy-start(f32[384]{0:T(512)} %param.33) | copy-start | bytes 4612
  9.1 20.2 %copy-start.24 = (f32[1024]{0:T(1024)}, f32[1024]{0:T(1024)S(1)}, u32[]{:S(2)}) copy-start(f32[1024]{0:T(1024)S(1)} %broadcast_multiply_fusion.4) | copy-start | bytes 12292
  11.2 18.2 %copy-start.35 = (f32[1024]{0:T(1024)}, f32[1024]{0:T(1024)S(1)}, u32[]{:S(2)}) copy-start(f32[1024]{0:T(1024)S(1)} %add_rsqrt_fusion) | copy-start | bytes 12292
  20.2 9.3 copy-start.9
  27.8 1.6 copy-start.11
  29.5 3.1 copy-start.32
  30.4 2.1 copy-start.21
  30.4 10.7 copy-start.50
  32.5 128.5 %all-gather.12.cloned.1.call-start = ((), (), s32[]{:S(2)}) async-start(), calls=%async_computation.14 | async-start | bytes 3932160 | tf_op jit(solution)/shard_map/all_gather | solution.py:174
  42.9 475.3 %all-gather.8.cloned.1.call-start = ((), (), s32[]{:S(2)}) async-start(), calls=%async_computation.9 | async-start | bytes 2949120 | tf_op jit(solution)/shard_map/all_gather | solution.py:143
  43.7 18.3 %copy-start.33 = (bf16[384,192]{0,1:T(8,128)(2,1)S(1)}, bf16[384,192]{0,1:T(8,128)(2,1)}, u32[]{:S(2)}) copy-start(bf16[384,192]{0,1:T(8,128)(2,1)} %param.35) | copy-start | bytes 442372
  43.7 497.3 %all-gather.10.cloned.1.call-start = ((), (), s32[]{:S(2)}) async-start(), calls=%async_computation.10 | async-start | bytes 2949120 | tf_op jit(solution)/shard_map/all_gather | solution.py:147
  44.3 26.2 %copy-start.17 = (bf16[1,1024,768]{2,1,0:T(8,128)(2,1)S(1)}, bf16[1,1024,768]{2,1,0:T(8,128)(2,1)}, u32[]{:S(2)}) copy-start(bf16[1,1024,768]{2,1,0:T(8,128)(2,1)} %param.41) | copy-start | bytes 4718596
  44.3 582.9 %reduce-scatter.9.cloned.1.call-start = ((), (), s32[]{:S(2)}) async-start(), calls=%async_computation.12 | async-start | bytes 7864320 | tf_op jit(solution)/shard_map/reduce_scatter | solution.py:244
  173.0 5.7 copy-start
  192.3 6.2 copy-start
  212.1 5.7 copy-start
  231.3 5.7 copy-start
  250.6 5.7 copy-start
  269.8 5.7 copy-start
  517.5 223.1 %reduce-scatter.11.cloned.1.call-start = ((), (), s32[]{:S(2)}) async-start(), calls=%async_computation.13 | async-start | bytes 7864320 | tf_op jit(solution)/shard_map/reduce_scatter | solution.py:245
  517.6 1.4 copy-start.2
  517.6 1.4 copy-start.25
  517.6 1.4 copy-start.36
  517.6 1.4 copy-start.42
  517.6 1.4 copy-start.46
  517.6 1.4 copy-start.47
  518.1 20.9 %copy-start.5 = (bf16[6,1024,64]{1,2,0:T(8,128)(2,1)S(1)}, bf16[6,1024,64]{1,2,0:T(8,128)(2,1)}, u32[]{:S(2)}) copy-start(bf16[6,1024,64]{1,2,0:T(8,128)(2,1)} %get-tuple-element.120) | copy-start | bytes 2359300
  518.1 247.6 %reduce-scatter.19.cloned.1.call-start = ((), (), s32[]{:S(2)}) async-start(), calls=%async_computation.18 | async-start | bytes 737280 | tf_op jit(solution)/shard_map/reduce_scatter | solution.py:308
  519.0 20.0 %copy-start.18 = (bf16[1,1024,768]{2,1,0:T(8,128)(2,1)S(1)}, bf16[1,1024,768]{2,1,0:T(8,128)(2,1)}, u32[]{:S(2)}) copy-start(bf16[1,1024,768]{2,1,0:T(8,128)(2,1)} %param.41) | copy-start | bytes 4718596
  540.9 260.4 %reduce-scatter.21.cloned.1.call-start = ((), (), s32[]{:S(2)}) async-start(), calls=%async_computation.19 | async-start | bytes 2949120 | tf_op jit(solution)/shard_map/reduce_scatter | solution.py:303
  551.4 1.6 copy-start.51
  553.0 4.3 copy-start.19
  557.2 279.9 %reduce-scatter.23.cloned.1.call-start = ((), (), s32[]{:S(2)}) async-start(), calls=%async_computation.20 | async-start | bytes 2949120 | tf_op jit(solution)/shard_map/reduce_scatter | solution.py:311
  557.3 6.3 copy-start.38
  557.3 6.3 copy-start.41
  563.2 65.5 %copy-start.23 = (f32[1024,8]{0,1:T(8,128)S(1)}, f32[1024,8]{0,1:T(8,128)}, u32[]{:S(2)}) copy-start(f32[1024,8]{0,1:T(8,128)} %copy-done.22) | copy-start | bytes 98308
  563.2 65.5 %copy-start.34 = (f32[1024,8]{0,1:T(8,128)S(1)}, f32[1024,8]{0,1:T(8,128)}, u32[]{:S(2)}) copy-start(f32[1024,8]{0,1:T(8,128)} %get-tuple-element.253) | copy-start | bytes 98308
  563.2 299.0 %reduce-scatter.13.cloned.1.call-start = ((), (), s32[]{:S(2)}) async-start(), calls=%async_computation.15 | async-start | bytes 737280 | tf_op jit(solution)/shard_map/reduce_scatter | solution.py:294
  627.1 4.0 copy-start.20
  633.0 253.8 %reduce-scatter.15.cloned.1.call-start = ((), (), s32[]{:S(2)}) async-start(), calls=%async_computation.16 | async-start | bytes 737280 | tf_op jit(solution)/shard_map/reduce_scatter | solution.py:297
  636.4 274.9 %reduce-scatter.17.cloned.1.call-start = ((), (), s32[]{:S(2)}) async-start(), calls=%async_computation.17 | async-start | bytes 737280 | tf_op jit(solution)/shard_map/reduce_scatter | solution.py:300
  744.4 247.2 %all-reduce.9.cloned.1.call-start = ((), (), s32[]{:S(2)}) async-start(), calls=%async_computation.21 | async-start | bytes 3538944 | tf_op jit(solution)/shard_map/psum | solution.py:286
  911.3 6.5 copy-start.12
  911.3 168.0 %all-reduce.11.cloned.1.call-start = ((), (), s32[]{:S(2)}) async-start(), calls=%async_computation.22 | async-start | bytes 6291456 | tf_op jit(solution)/shard_map/psum | solution.py:274
  919.1 1.6 copy-start.3
  919.1 1.7 copy-start.14
  923.0 244.8 %all-reduce.7.cloned.1.call-start = ((), (), s32[]{:S(2)}) async-start(), calls=%async_computation.11 | async-start | bytes 6291456 | tf_op jit(solution)/shard_map/psum | solution.py:202
  923.3 5.4 copy-start.6
  923.3 5.4 copy-start.16
  991.6 4.5 copy-start.29
  991.6 5.2 copy-start.28
  991.6 6.0 copy-start.27
  991.6 6.7 copy-start.26
  996.8 171.1 %copy-start.43 = (f32[768]{0:T(1024)S(1)}, f32[768]{0:T(1024)}, u32[]{:S(2)}) copy-start(f32[768]{0:T(1024)} %param.40) | copy-start | bytes 9220
  996.8 171.1 %copy-start.44 = (f32[768]{0:T(1024)S(1)}, f32[768]{0:T(1024)}, u32[]{:S(2)}) copy-start(f32[768]{0:T(1024)} %param.36) | copy-start | bytes 9220
  1079.3 88.5 %copy-start.4 = (bf16[1024,768]{1,0:T(8,128)(2,1)S(1)}, bf16[1024,768]{1,0:T(8,128)(2,1)}, u32[]{:S(2)}) copy-start(bf16[1024,768]{1,0:T(8,128)(2,1)} %get-tuple-element.226) | copy-start | bytes 4718596
  (8 other events, 7.6 us)
Sparse Core Ops, SparseCore 0:
  32.6 64.5 all-gather.5
  98.7 62.1 all-gather.11
  162.5 22.7 all-gather.7
  186.7 24.0 all-gather.9
  517.7 109.4 reduce-scatter.8
  629.3 111.2 reduce-scatter.10
  743.1 22.5 reduce-scatter.18
  768.3 33.0 reduce-scatter.20
  804.1 33.0 reduce-scatter.22
  840.1 22.0 reduce-scatter.12
  864.7 22.0 reduce-scatter.14
  889.2 22.0 reduce-scatter.16
  914.1 77.4 all-reduce.8
  994.5 84.7 all-reduce.10
  1082.1 85.7 all-reduce.6
where the time goes:
time: 1250 us; the launch traced here: 1240 us
  waiting for transfers between devices  639 us (51%)
  matrix products  339 us (27%)
  blocking collectives  108 us (9%)
  other arithmetic  104 us (8%)
  local copies, waits for them, and re-layouts  36.1 us (3%)
  between operations  14.8 us (1%)
    reduce_scatter x1, waiting for transfers between devices, body(): lax.psum_scatter(grad_value_all, 'context', scatter_dimension=1, tiled=True)  104 us
    psum x1, waiting for transfers between devices, body(): summed = lax.psum(partial_out, 'tensor')  84.1 us
    dot_general x12, matrix products, item_scores(): jnp.einsum('qd,kd->qk', query_item, key_item, preferred_element_type=jnp....  82.6 us
    psum x1, waiting for transfers between devices, body(): lax.psum(back_two.astype(jnp.bfloat16), 'tensor').astype(jnp.float32)  80.3 us
    psum x1, blocking collectives, body(): lax.psum((grad_g1, grad_s1, grad_g2, grad_s2, grad_qb, grad_kb, grad_vb,...  62.1 us
    reduce_scatter x1, waiting for transfers between devices, body(): lax.psum_scatter(grad_key_all, 'context', scatter_dimension=1, tiled=True)  60.3 us
    psum x1, waiting for transfers between devices, body(): lax.psum(grad_wq.astype(jnp.bfloat16), 'context').astype(jnp.float32)  59.9 us
    all_gather x1, waiting for transfers between devices, body(): lax.all_gather(value_low.reshape(seq_count, block_len, part_width), 'cont...  57.2 us
  transfers between devices with their start and end apart: 15, of which 13 were waited for; matrix products, arithmetic and copies ran while one was open for 36% of the time, Pallas kernels for 0%

commit v1 on v0

v1 whole, which is shorter than its diff:
```python
import math

import jax
import jax.numpy as jnp
from jax import lax
from jax.experimental import pallas as pl
from jax.experimental.pallas import tpu as pltpu
from jax.sharding import PartitionSpec as P

HEAD_DIM = 64
ROT_DIM = 16


epsilon = 1e-05


def rotary_tables(places):
    frequency = jnp.exp(
        jnp.arange(ROT_DIM // 2, dtype=jnp.float32) * (-2.0 * math.log(10000.0) / ROT_DIM)
    )
    angle_rad = places.astype(jnp.float32)[..., None] * frequency
    return (jnp.cos(angle_rad), jnp.sin(angle_rad))


def rotate_rows(field, cosine, sine):
    half_rot = ROT_DIM // 2
    width, row_count = field.shape
    heads = field.reshape(width // HEAD_DIM, HEAD_DIM, row_count)
    leading = heads[:, :half_rot]
    trailing = heads[:, half_rot:ROT_DIM]
    return jnp.concatenate(
        [
            leading * cosine - trailing * sine,
            trailing * cosine + leading * sine,
            heads[:, ROT_DIM:],
        ],
        axis=1,
    ).reshape(width, row_count)


def normalize(values):
    row_mean = jnp.mean(values, axis=-1, keepdims=True)
    centred = values - row_mean
    row_var = jnp.mean(centred * centred, axis=-1, keepdims=True)
    inv_std = lax.rsqrt(row_var + epsilon)
    return (centred * inv_std, inv_std)


def fold_rows(field, how):
    rows, lanes = field.shape
    return how(field.reshape(rows // 8, 8, lanes), axis=0)


def attend_kernel(
    query_places,
    key_places,
    query_ref,
    key_ref,
    value_ref,
    grad_ref,
    mixed_ref,
    grad_query_ref,
    grad_key_ref,
    grad_value_ref,
    key_rows,
    value_rows,
    key_sum,
    value_sum,
    score_buf,
    prob_buf,
):
    chunks, chunk_len, query_len = score_buf.shape
    block = pl.program_id(2)

    @pl.when(block == 0)
    def _():
        def turn(c, carry):
            key_rows[c] = key_ref[c].T
            value_rows[c] = value_ref[c].T
            key_sum[c] = jnp.zeros_like(key_sum[c])
            value_sum[c] = jnp.zeros_like(value_sum[c])
            return carry

        lax.fori_loop(0, chunks, turn, 0)

    scale = HEAD_DIM ** (-0.5)
    query = query_ref[...]
    grad = grad_ref[...]
    query_scaled = query * jnp.bfloat16(scale)
    own_places = query_places[0]

    def score_step(c, top):
        scores = jnp.dot(key_rows[c], query_scaled, preferred_element_type=jnp.float32)
        places = jnp.concatenate([key_places[c]] * (query_len // 128), axis=1)
        scores = jnp.where(places <= own_places, scores, -1e30)
        score_buf[c] = scores
        return jnp.maximum(top, fold_rows(scores, jnp.max))

    top = lax.fori_loop(
        0, chunks, score_step, jnp.full((8, query_len), -1e30, jnp.float32)
    )
    row_max = jnp.max(top, axis=0, keepdims=True)

    def prob_step(c, carry):
        total, mixed = carry
        probs = jnp.exp(score_buf[c] - row_max)
        low = probs.astype(jnp.bfloat16)
        prob_buf[c] = low
        mixed = mixed + jnp.dot(value_ref[c], low, preferred_element_type=jnp.float32)
        return total + fold_rows(probs, jnp.sum), mixed

    total, mixed = lax.fori_loop(
        0,
        chunks,
        prob_step,
        (
            jnp.zeros((8, query_len), jnp.float32),
            jnp.zeros((HEAD_DIM, query_len), jnp.float32),
        ),
    )
    inverse = 1.0 / jnp.sum(total, axis=0, keepdims=True)
    mixed = mixed * inverse
    mixed_ref[...] = mixed.astype(jnp.bfloat16)
    delta = jnp.sum(mixed * grad.astype(jnp.float32), axis=0, keepdims=True)
    query_back = (query.astype(jnp.float32) * (inverse * scale)).T.astype(jnp.bfloat16)
    grad_back = (grad.astype(jnp.float32) * inverse).T.astype(jnp.bfloat16)

    def back_step(c, grad_query):
        low = prob_buf[c]
        grad_probs = jnp.dot(value_rows[c], grad, preferred_element_type=jnp.float32)
        grad_scores = (low.astype(jnp.float32) * (grad_probs - delta)).astype(jnp.bfloat16)
        value_sum[c] += jnp.dot(low, grad_back, preferred_element_type=jnp.float32)
        key_sum[c] += jnp.dot(grad_scores, query_back, preferred_element_type=jnp.float32)
        return grad_query + jnp.dot(
            key_ref[c], grad_scores, preferred_element_type=jnp.float32
        )

    grad_query = lax.fori_loop(
        0, chunks, back_step, jnp.zeros((HEAD_DIM, query_len), jnp.float32)
    )
    grad_query_ref[...] = grad_query * (inverse * scale)

    @pl.when(block == pl.num_programs(2) - 1)
    def _():
        def turn(c, carry):
            grad_key_ref[c] = key_sum[c].T.astype(jnp.bfloat16)
            grad_value_ref[c] = value_sum[c].T.astype(jnp.bfloat16)
            return carry

        lax.fori_loop(0, chunks, turn, 0)


def attend(query, key_value, grad, own_places, all_places, seq_count, block_len):
    width, row_count = query.shape
    chunks = key_value.shape[0]
    heads = width // HEAD_DIM
    query_len = 512 if block_len % 512 == 0 else block_len
    blocks = block_len // query_len
    column_places = jnp.broadcast_to(
        all_places.reshape(chunks, row_count)[..., None], (chunks, row_count, 128)
    )
    row_places = own_places.reshape(row_count // query_len, 1, query_len)
    one = pl.BlockSpec((HEAD_DIM, query_len), lambda s, h, i: (h, s * blocks + i))
    every = pl.BlockSpec((chunks, HEAD_DIM, block_len), lambda s, h, i: (0, h, s))
    pairs = row_count * chunks * block_len * heads
    return pl.pallas_call(
        attend_kernel,
        grid=(seq_count, heads, blocks),
        in_specs=[
            pl.BlockSpec((1, 1, query_len), lambda s, h, i: (s * blocks + i, 0, 0)),
            pl.BlockSpec((chunks, block_len, 128), lambda s, h, i: (0, s, 0)),
            one,
            every,
            pl.BlockSpec((chunks, HEAD_DIM, block_len), lambda s, h, i: (0, h + heads, s)),
            one,
        ],
        out_specs=[one, one, every, every],
        out_shape=[
            jax.ShapeDtypeStruct((width, row_count), jnp.bfloat16),
            jax.ShapeDtypeStruct((width, row_count), jnp.float32),
            jax.ShapeDtypeStruct((chunks, width, row_count), jnp.bfloat16),
            jax.ShapeDtypeStruct((chunks, width, row_count), jnp.bfloat16),
        ],
        scratch_shapes=[
            pltpu.VMEM((chunks, block_len, HEAD_DIM), jnp.bfloat16),
            pltpu.VMEM((chunks, block_len, HEAD_DIM), jnp.bfloat16),
            pltpu.VMEM((chunks, block_len, HEAD_DIM), jnp.float32),
            pltpu.VMEM((chunks, block_len, HEAD_DIM), jnp.float32),
            pltpu.VMEM((chunks, block_len, query_len), jnp.float32),
            pltpu.VMEM((chunks, block_len, query_len), jnp.bfloat16),
        ],
        compiler_params=pltpu.CompilerParams(vmem_limit_bytes=50 * 2**20),
        cost_estimate=pl.CostEstimate(
            flops=48 * pairs * HEAD_DIM, bytes_accessed=32 * 2**20, transcendentals=pairs
        ),
    )(row_places, column_places, query, key_value, key_value, grad)


def over_tensor(part):
    low = part.astype(jnp.bfloat16)
    count = lax.axis_size("tensor")
    if count != 2:
        return lax.psum(low, "tensor").astype(jnp.float32)
    other = lax.ppermute(low, "tensor", [(0, 1), (1, 0)])
    return low.astype(jnp.float32) + other.astype(jnp.float32)


def owner_sum(grads):
    own = lax.psum_scatter(grads.astype(jnp.bfloat16), "dp", scatter_dimension=0, tiled=True)
    return lax.psum(own, "context").astype(jnp.float32)


def body(
    tokens,
    positions,
    first_gain,
    first_shift,
    second_gain,
    second_shift,
    w_query,
    w_key,
    w_value,
    query_bias,
    key_bias,
    value_bias,
    w_out,
    out_bias,
    w_up,
    up_bias,
    w_down,
    down_bias,
    cotangent,
):
    seq_count, block_len, model_width = tokens.shape
    row_count = seq_count * block_len
    flat_in = tokens.reshape(row_count, model_width).astype(jnp.float32)
    upstream = cotangent.reshape(row_count, model_width)
    ff_part = w_up.shape[1]
    part_width = w_query.shape[1]
    half_rot = ROT_DIM // 2
    f32 = jnp.float32
    low = jnp.bfloat16

    def mm(spec, left, right):
        return jnp.einsum(spec, left, right, preferred_element_type=f32)

    full_qkv = lax.all_gather(
        jnp.concatenate([w_query, w_key, w_value], axis=1), "dp", axis=0, tiled=True
    )
    places = lax.all_gather(positions, "context", axis=0, tiled=False)
    full_rest = lax.all_gather(
        jnp.concatenate([w_up, w_down.T, w_out.T], axis=1), "dp", axis=0, tiled=True
    )
    full_up = full_rest[:, :ff_part]
    full_down = full_rest[:, ff_part : 2 * ff_part]
    full_out = full_rest[:, 2 * ff_part :]

    plain, inv_std = normalize(flat_in)
    normed_one = (plain * first_gain + first_shift).astype(low)
    normed_two = (plain * second_gain + second_shift).astype(low)
    cosine, sine = rotary_tables(positions)
    cosine = cosine.reshape(row_count, half_rot).T
    sine = sine.reshape(row_count, half_rot).T

    qkv_bias = jnp.concatenate([query_bias, key_bias, value_bias])
    qkv = mm("dc,rd->cr", full_qkv, normed_one) + qkv_bias[:, None]
    query = rotate_rows(qkv[:part_width], cosine, sine).astype(low)
    key = rotate_rows(qkv[part_width : 2 * part_width], cosine, sine).astype(low)
    value = qkv[2 * part_width :].astype(low)
    key_value = lax.all_gather(
        jnp.concatenate([key, value], axis=0), "context", axis=0, tiled=False
    )

    grad_mixed = mm("dc,rd->cr", full_out, upstream).astype(low)
    inner = mm("rd,df->rf", normed_two, full_up) + up_bias
    below = 0.5 * (1.0 + lax.erf(inner * (0.5**0.5)))
    hidden = (inner * below).astype(low)
    slope = below + inner * jnp.exp(-0.5 * inner * inner) * ((2.0 * math.pi) ** -0.5)
    grad_inner = (mm("rd,df->rf", upstream, full_down) * slope).astype(low)
    grad_ff = jnp.concatenate(
        [mm("rd,rf->df", normed_two, grad_inner), mm("rd,rf->df", upstream, hidden)], axis=1
    )
    own_ff = owner_sum(grad_ff)
    back_two = mm("rf,df->rd", grad_inner, full_up)
    out_two = mm("rf,df->rd", hidden, full_down)
    upstream_wide = upstream.astype(f32)

    mixed, grad_query_rot, grad_key_all, grad_value_all = attend(
        query, key_value, grad_mixed, positions, places, seq_count, block_len
    )
    key_part = lax.psum_scatter(grad_key_all, "context", scatter_dimension=0, tiled=False)
    value_part = lax.psum_scatter(grad_value_all, "context", scatter_dimension=0, tiled=False)

    summed = over_tensor(mm("cr,dc->rd", mixed, full_out) + out_two)
    block_out = (
        (flat_in + summed + out_bias + down_bias)
        .astype(low)
        .reshape(seq_count, block_len, model_width)
    )

    grad_qkv = jnp.concatenate(
        [
            rotate_rows(grad_query_rot, cosine, -sine).astype(low),
            rotate_rows(key_part.astype(f32), cosine, -sine).astype(low),
            value_part,
        ],
        axis=0,
    )
    back_one = mm("cr,dc->rd", grad_qkv, full_qkv)
    tilted = over_tensor(back_one * first_gain + back_two * second_gain)
    first_mean = jnp.mean(tilted, axis=-1, keepdims=True)
    second_mean = jnp.mean(tilted * plain, axis=-1, keepdims=True)
    grad_tokens = (
        upstream_wide + inv_std * (tilted - first_mean - plain * second_mean)
    ).reshape(seq_count, block_len, model_width)

    grad_late = jnp.concatenate(
        [mm("rd,cr->dc", upstream, mixed), mm("rd,cr->dc", normed_one, grad_qkv)], axis=1
    )
    own_late = owner_sum(grad_late)

    gains = jnp.stack(
        [
            jnp.sum(back_one * plain, axis=0),
            jnp.sum(back_one, axis=0),
            jnp.sum(back_two * plain, axis=0),
            jnp.sum(back_two, axis=0),
        ]
    ).reshape(-1)
    biases = jnp.concatenate(
        [
            jnp.sum(grad_qkv.astype(f32), axis=1),
            jnp.sum(grad_inner.astype(f32), axis=0),
            jnp.sum(upstream_wide, axis=0),
        ]
    )
    vectors = lax.all_gather(
        jnp.concatenate([gains, biases]), ("tensor", "dp", "context"), axis=0, tiled=False
    )
    sum_g1, sum_s1, sum_g2, sum_s2 = jnp.sum(vectors[:, : gains.shape[0]], axis=0).reshape(
        4, model_width
    )
    sides = lax.axis_size("tensor")
    own_side = lax.dynamic_index_in_dim(
        vectors[:, gains.shape[0] :].reshape(sides, -1, biases.shape[0]),
        lax.axis_index("tensor"),
        0,
        keepdims=False,
    )
    sum_b = jnp.sum(own_side, axis=0)
    cuts = [part_width, 2 * part_width, 3 * part_width, 3 * part_width + ff_part]
    sum_qb, sum_kb, sum_vb, sum_ub, sum_ob = jnp.split(sum_b, cuts)
    shard_out, shard_query, shard_key, shard_value = jnp.split(own_late, 4, axis=1)
    shard_up = own_ff[:, :ff_part]
    shard_down = own_ff[:, ff_part:].T
    shard_out = shard_out.T
    return (
        block_out,
        grad_tokens,
        sum_g1,
        sum_s1,
        sum_g2,
        sum_s2,
        shard_query,
        shard_key,
        shard_value,
        sum_qb,
        sum_kb,
        sum_vb,
        shard_out,
        sum_ob,
        shard_up,
        sum_ub,
        shard_down,
        sum_ob,
    )


def solution(mesh):
    return jax.shard_map(
        body,
        mesh=mesh,
        in_specs=(
            P("dp", "context", None),
            P("dp", "context"),
            P(),
            P(),
            P(),
            P(),
            P("dp", "tensor"),
            P("dp", "tensor"),
            P("dp", "tensor"),
            P("tensor"),
            P("tensor"),
            P("tensor"),
            P("tensor", "dp"),
            P(),
            P("dp", "tensor"),
            P("tensor"),
            P("tensor", "dp"),
            P(),
            P("dp", "context", None),
        ),
        out_specs=(
            P("dp", "context", None),
            P("dp", "context", None),
            P(),
            P(),
            P(),
            P(),
            P("dp", "tensor"),
            P("dp", "tensor"),
            P("dp", "tensor"),
            P("tensor"),
            P("tensor"),
            P("tensor"),
            P("tensor", "dp"),
            P(),
            P("dp", "tensor"),
            P("tensor"),
            P("tensor", "dp"),
            P(),
        ),
        check_vma=False,
    )
```

time: 1250 us -> 629 us (0.50)
  waiting for transfers between devices: 639 us -> 305 us
  matrix products: 339 us -> 47.8 us
  Pallas kernels: 0 us -> 113 us
  other arithmetic: 104 us -> 28.4 us
  local copies, waits for them, and re-layouts: 36.1 us -> 16.4 us
    dot_general x60 -> x12, matrix products: 339 us -> 47.8 us  [mm(): return jnp.einsum(spec, left, right, preferred_element_type=f32)]
    psum x3 -> x1, waiting for transfers between devices: 224 us -> 0.01 us  [owner_sum(): return lax.psum(own, 'context').astype(jnp.float32)]
    reduce_scatter x8 -> x4, waiting for transfers between devices: 331 us -> 115 us  [the longest x1 58.7 us: body(): lax.psum_scatter(grad_value_all, 'context', scatter_dimension=0, tiled=Fa...]
    pallas_call x0 -> x1, Pallas kernels: none -> 113 us  [attend(): pl.pallas_call(attend_kernel, grid=(seq_count, heads, blocks), in_specs=[...]
    all_gather x4 -> x3, waiting for transfers between devices: 81.6 us -> 158 us  [the longest x1 114 us: body(): lax.all_gather(jnp.concatenate([key, value], axis=0), 'context', axis=0,...]
    psum x1 -> x0, blocking collectives: 62.1 us -> none  [body(): lax.psum((grad_g1, grad_s1, grad_g2, grad_s2, grad_qb, grad_kb, grad_vb,...]
    all_gather x5 -> x2, blocking collectives: 45.5 us -> 100 us  [the longest x1 87.1 us: body(): lax.all_gather(jnp.concatenate([gains, biases]), ('tensor', 'dp', 'contex...]
    convert_element_type x14 -> x3, other arithmetic: 57.2 us -> 2.73 us  [the longest x2 1.43 us: owner_sum(): return lax.psum(own, 'context').astype(jnp.float32)]
  transfers between devices with their start and end apart: 15 -> 10, of which waited for: 13 -> 8; matrix products, arithmetic and copies ran while one was open for 36% -> 12% of each run, Pallas kernels for 0% -> 0%
where the time goes in v1:
time: 629 us; the launch traced here: 628 us
  waiting for transfers between devices  305 us (48%)
  Pallas kernels  113 us (18%)
  blocking collectives  100 us (16%)
  matrix products  47.8 us (8%)
  other arithmetic  28.4 us (5%)
  local copies, waits for them, and re-layouts  16.4 us (3%)
  between operations  14.8 us (2%)
    all_gather x1, waiting for transfers between devices, body(): lax.all_gather(jnp.concatenate([key, value], axis=0), 'context', axis=0,...  114 us
    pallas_call x1, Pallas kernels, attend(): pl.pallas_call(attend_kernel, grid=(seq_count, heads, blocks), in_specs=[...  113 us
    all_gather x1, blocking collectives, body(): lax.all_gather(jnp.concatenate([gains, biases]), ('tensor', 'dp', 'contex...  87.1 us
    reduce_scatter x1, waiting for transfers between devices, body(): lax.psum_scatter(grad_value_all, 'context', scatter_dimension=0, tiled=Fa...  58.7 us
    dot_general x12, matrix products, mm(): return jnp.einsum(spec, left, right, preferred_element_type=f32)  47.8 us
    reduce_scatter x1, waiting for transfers between devices, body(): lax.psum_scatter(grad_key_all, 'context', scatter_dimension=0, tiled=False)  32 us
    ppermute x2, waiting for transfers between devices, over_tensor(): other = lax.ppermute(low, 'tensor', [(0, 1), (1, 0)])  30.8 us
    reduce_scatter x2, waiting for transfers between devices, owner_sum(): lax.psum_scatter(grads.astype(jnp.bfloat16), 'dp', scatter_dimension=0, t...  24.8 us
  transfers between devices with their start and end apart: 10, of which 8 were waited for; matrix products, arithmetic and copies ran while one was open for 12% of the time, Pallas kernels for 0%

profile of v1, /device:TPU:0, one launch (start us, length us, event | category | flops | bytes accessed | tf_op | source)
XLA Modules:
  0.0 628.5 jit_solution(6479604114004624560)
XLA Ops:
  7.3 2.0 pad_maximum_fusion.9
  9.4 2.5 pad_maximum_fusion.4
  12.0 0.3 convert_reduce_fusion.3
  12.3 0.6 fusion.25
  12.9 0.2 fusion.57
  13.1 20.6 %all-gather.9.cloned.1.call-done = bf16[768,1152]{1,0:T(8,128)(2,1)} async-done(((bf16[192,1152]{1,0:T(8,128)(2,1)}), bf16[768,1152]{1,0:T(8,128)(2,1)}) %all-gather.9.cloned.1.call-update) | async-done | bytes 1769488 | tf_op jit(solution)/shard_map/all_gather | solution.py:247
  33.7 4.2 convolution_add_fusion
  37.9 0.1 slice.153
  38.0 0.3 fusion.63
  38.3 0.1 slice.155
  38.4 0.1 subtract_convert_fusion.2
  38.5 0.1 pad_maximum_fusion.6
  38.6 1.3 pad_maximum_fusion.3
  39.9 13.2 %all-gather.3 = s32[4,1,1024]{2,1,0:T(1,128)S(1)} all-gather(s32[1,1,1024]{2,1,0:T(1,128)S(1)} %bitcast.126), channel_id=2, replica_groups=mesh['dp'=4,'context'=4,'tensor'=2] {'context'}, dimensions={0}, use_global_device_ids=true | all-gather | bytes 20480 | tf_op jit(solution)/shard_map/all_gather | solution.py:250
  53.1 0.1 slice.156
  53.3 23.4 %all-gather.11.cloned.1.call-done = bf16[768,3456]{1,0:T(8,128)(2,1)} async-done(((bf16[192,3456]{1,0:T(8,128)(2,1)}), bf16[768,3456]{1,0:T(8,128)(2,1)}) %all-gather.11.cloned.1.call-update) | async-done | bytes 5308432 | tf_op jit(solution)/shard_map/all_gather | solution.py:251
  76.7 3.3 fusion.46.grad_ref
  80.0 114.2 %all-gather.13.cloned.1.call-done = bf16[3072,1024]{1,0:T(8,128)(2,1)} async-done(((bf16[768,1024]{1,0:T(8,128)(2,1)}), bf16[3072,1024]{1,0:T(8,128)(2,1)}) %all-gather.13.cloned.1.call-update) | async-done | bytes 6291472 | tf_op jit(solution)/shard_map/all_gather | solution.py:270
  194.2 2.2 broadcast_in_dim.5.key_places
  196.4 1.1 copy-done.1
  197.6 113.0 %shard_map.322 = (bf16[384,1024]{1,0:T(8,128)(2,1)S(1)}, f32[384,1024]{1,0:T(8,128)S(1)}, bf16[4,384,1024]{2,1,0:T(8,128)(2,1)}, bf16[4,384,1024]{2,1,0:T(8,128)(2,1)}) custom-call(s32[2,1,512]{2,1,0:T(1,128)S(1)} %bitcast.127, s32[4,1024,128]{2,1,0:T(8,128)} %broadcast_in_dim.5.key_places, bf16[384,1024]{1,0:T(8,128)(2,1)S(1)} %bitcast.123, ...), custom_call_target="tpu_custom_call" | custom-call | flops 77309411328 | bytes 33554432 | tf_op jit(solution)/shard_map/pallas_call | solution.py:166
  310.6 0.5 reduce-scatter.7.cloned.1.call-update
  311.2 0.2 reduce-scatter.11.cloned.1.call-start
  311.4 5.4 multiply_convert_fusion
  316.8 2.9 fusion.30
  319.7 5.6 convert_reduce_fusion
  325.4 1.7 copy-done.21
  327.1 3.1 convolution_convert_fusion.1
  330.2 2.8 pad_maximum_fusion
  333.1 0.9 slice.154
  334.0 2.2 fusion.52
  336.2 1.1 copy.39
  337.2 32.0 %reduce-scatter.5.cloned.1.call-done = bf16[1,384,1024]{2,1,0:T(8,128)(2,1)} async-done(((bf16[4,384,1024]{2,1,0:T(8,128)(2,1)}), bf16[1,384,1024]{2,1,0:T(8,128)(2,1)}) %reduce-scatter.5.cloned.1.call-update) | async-done | bytes 786448 | tf_op jit(solution)/shard_map/reduce_scatter | solution.py:291
  369.2 1.3 convert_element_type.101
  370.5 1.1 slice.114
  371.6 0.1 subtract_convert_fusion.1
  371.7 1.2 pad_maximum_fusion.7
  373.0 58.7 %reduce-scatter.7.cloned.1.call-done = bf16[1,384,1024]{2,1,0:T(8,128)(2,1)} async-done(((bf16[4,384,1024]{2,1,0:T(8,128)(2,1)}), bf16[1,384,1024]{2,1,0:T(8,128)(2,1)}) %reduce-scatter.7.cloned.1.call-update) | async-done | bytes 786448 | tf_op jit(solution)/shard_map/reduce_scatter | solution.py:292
  431.7 4.4 convolution_convert_fusion.2
  436.1 1.6 pad_maximum_fusion.2
  437.7 0.3 all-reduce.3.cloned.1.call-start
  438.0 4.6 fusion.58
  442.6 7.3 %add_convert_fusion = (bf16[1024,768]{1,0:T(8,128)(2,1)}, f32[1024,768]{1,0:T(8,128)}) fusion(f32[1024,768]{1,0:T(8,128)S(1)} %fusion.58, f32[768]{0:T(1024)S(1)} %copy-done.20, f32[768]{0:T(1024)S(1)} %copy-done.19, bf16[1024,1536]{1,0:T(8,128)(2,1)S(1)} %copy-done.22, bf16[768,3456]{1,0:T(8,128)(2,1)} %all-gather.11.cloned.1.call-done), kind=kOutput, calls=%fused_computation.45 | convolution fusion | flops 2419064832 | bytes 13375488 | tf_op jit(solution)/shard_map/rf,df->rd/dot_general | solution.py:245
  450.0 1.2 collective-permute-start.1
  451.1 2.6 fusion.33
  453.8 2.2 add_convert_fusion.1
  456.0 0.9 collective-permute-start
  456.8 1.8 convert_reduce_fusion.1
  458.6 29.0 %collective-permute-done.1 = bf16[1024,768]{1,0:T(8,128)(2,1)} collective-permute-done((bf16[1024,768]{1,0:T(8,128)(2,1)}, bf16[1024,768]{1,0:T(8,128)(2,1)}, u32[]{:S(2)}, u32[]{:S(2)}) %collective-permute-start.1) | collective-permute-done | bytes 1572896 | tf_op jit(solution)/shard_map/ppermute | solution.py:204
  487.6 5.2 fusion.31
  493.0 24.8 %reduce-scatter.9.cloned.1.call-done = bf16[192,1536]{1,0:T(8,128)(2,1)} async-done(((bf16[768,1536]{1,0:T(8,128)(2,1)}), bf16[192,1536]{1,0:T(8,128)(2,1)}) %reduce-scatter.9.cloned.1.call-update) | async-done | bytes 589840 | tf_op jit(solution)/shard_map/reduce_scatter | solution.py:209
  517.8 1.8 collective-permute-done
  519.6 5.7 convert_reduce_fusion.2
  525.4 87.1 %all-gather.4 = f32[32,1,6528]{2,1,0:T(1,128)S(1)} all-gather(f32[1,1,6528]{2,1,0:T(1,128)S(1)} %reshape.182), channel_id=4, replica_groups=mesh['dp'=4,'context'=4,'tensor'=2] {'tensor','dp','context'}, dimensions={0}, use_global_device_ids=true | all-gather | bytes 861696 | tf_op jit(solution)/shard_map/all_gather | solution.py:337
  612.7 0.6 split.44
  613.3 0.6 fusion.65
  613.9 0.6 fusion.66
  614.5 2.1 fusion.64
  616.6 1.2 convert_element_type.109
  617.8 1.1 slice.117
  618.9 0.2 convert_element_type.110
  619.2 0.7 slice_bitcast_fusion.1
  619.9 1.1 slice_bitcast_fusion
  621.1 0.6 copy.51
  (90 shorter events, 0.9 us)
Async XLA Ops:
  7.2 4.7 copy-start
  7.2 4.8 copy-start.13
  7.2 4.8 copy-start.14
  7.2 4.8 copy-start.15
  7.2 4.8 copy-start.2
  7.2 26.5 %all-gather.9.cloned.1.call-start = ((), (), s32[]{:S(2)}) async-start(), calls=%async_computation.4 | async-start | bytes 2211840 | tf_op jit(solution)/shard_map/all_gather | solution.py:247
  9.3 67.4 %all-gather.11.cloned.1.call-start = ((), (), s32[]{:S(2)}) async-start(), calls=%async_computation.5 | async-start | bytes 6635520 | tf_op jit(solution)/shard_map/all_gather | solution.py:251
  9.3 24.4 %copy-start.18 = (f32[768]{0:T(1024)S(1)}, f32[768]{0:T(1024)}, u32[]{:S(2)}) copy-start(f32[768]{0:T(1024)} %param.22) | copy-start | bytes 9220
  9.3 24.4 %copy-start.19 = (f32[768]{0:T(1024)S(1)}, f32[768]{0:T(1024)}, u32[]{:S(2)}) copy-start(f32[768]{0:T(1024)} %param.21) | copy-start | bytes 9220
  11.9 182.3 %all-gather.13.cloned.1.call-start = ((), (), s32[]{:S(2)}) async-start(), calls=%async_computation.10 | async-start | bytes 7864320 | tf_op jit(solution)/shard_map/all_gather | solution.py:270
  39.9 329.3 %reduce-scatter.5.cloned.1.call-start = ((), (), s32[]{:S(2)}) async-start(), calls=%async_computation.6 | async-start | bytes 3932160 | tf_op jit(solution)/shard_map/reduce_scatter | solution.py:291
  196.4 1.1 copy-start.1
  310.5 0.9 copy-start.16
  310.5 0.9 copy-start.17
  310.5 0.9 copy-start.20
  310.6 121.1 %reduce-scatter.7.cloned.1.call-start = ((), (), s32[]{:S(2)}) async-start(), calls=%async_computation.7 | async-start | bytes 3932160 | tf_op jit(solution)/shard_map/reduce_scatter | solution.py:292
  311.2 181.8 %reduce-scatter.11.cloned.1.call-start = ((), (), s32[]{:S(2)}) async-start(), calls=%async_computation.9 | async-start | bytes 5898240 | tf_op jit(solution)/shard_map/reduce_scatter | solution.py:209
  311.4 5.4 copy-start.9
  316.8 2.9 copy-start.23
  319.7 7.3 %copy-start.3 = (bf16[1,1024,768]{2,1,0:T(8,128)(2,1)S(1)}, bf16[1,1024,768]{2,1,0:T(8,128)(2,1)}, u32[]{:S(2)}) copy-start(bf16[1,1024,768]{2,1,0:T(8,128)(2,1)} %param.19) | copy-start | bytes 4718596
  325.4 1.7 copy-start.21
  333.0 184.7 %reduce-scatter.9.cloned.1.call-start = ((), (), s32[]{:S(2)}) async-start(), calls=%async_computation.8 | async-start | bytes 2949120 | tf_op jit(solution)/shard_map/reduce_scatter | solution.py:209
  373.0 65.0 %copy-start.7 = (bf16[6,64,1024]{2,1,0:T(8,128)(2,1)}, bf16[6,64,1024]{2,1,0:T(8,128)(2,1)S(1)}, u32[]{:S(2)}) copy-start(bf16[6,64,1024]{2,1,0:T(8,128)(2,1)S(1)} %get-tuple-element.75) | copy-start | bytes 2359300
  431.7 4.4 copy-start.8
  437.7 176.8 %all-reduce.3.cloned.1.call-start = ((), (), s32[]{:S(2)}) async-start(), calls=%async_computation.11 | async-start | bytes 3538944 | tf_op jit(solution)/shard_map/psum | solution.py:210
  438.0 4.6 copy-start.22
  438.0 13.1 %slice-start = ((s8[5308416]{0:T(1024)(128)(4,1)}), s8[4194304]{0:T(1024)(128)(4,1)S(1)}, s32[]{:S(2)}) async-start(s8[5308416]{0:T(1024)(128)(4,1)} %bitcast.150), calls=%async_computation.12 | async-start | bytes 8388608
  442.6 7.4 %copy-start.6 = (f32[1024,768]{1,0:T(8,128)}, f32[1024,768]{1,0:T(8,128)S(1)}, u32[]{:S(2)}) copy-start(f32[1024,768]{1,0:T(8,128)S(1)} %fusion.58) | copy-start | bytes 9437188
  442.6 8.5 %slice-start.1 = ((s8[5308416]{0:T(1024)(128)(4,1)}), s8[1114112]{0:T(1024)(128)(4,1)S(1)}, s32[]{:S(2)}) async-start(s8[5308416]{0:T(1024)(128)(4,1)} %bitcast.150), calls=%async_computation.13 | async-start | bytes 2228224
  442.6 8.5 %copy-start.24 = (bf16[1024,1536]{1,0:T(8,128)(2,1)S(1)}, bf16[1024,1536]{1,0:T(8,128)(2,1)}, u32[]{:S(2)}) copy-start(bf16[1024,1536]{1,0:T(8,128)(2,1)} %copy-done.23) | copy-start | bytes 9437188
  450.0 37.6 %collective-permute-start.1 = (bf16[1024,768]{1,0:T(8,128)(2,1)}, bf16[1024,768]{1,0:T(8,128)(2,1)}, u32[]{:S(2)}, u32[]{:S(2)}) collective-permute-start(bf16[1024,768]{1,0:T(8,128)(2,1)} %get-tuple-element.68), channel_id=1, source_target_pairs={{0,1},{1,0},{2,3},{3,2},{4,5},{5,4},{6,7},{7,6},{8,9},{9,8},{10,11... | collective-permute-start | bytes 4718600 | tf_op jit(solution)/shard_map/ppermute | solution.py:204
  453.8 33.8 %copy-start.4 = (bf16[1,1024,768]{2,1,0:T(8,128)(2,1)S(1)}, bf16[1,1024,768]{2,1,0:T(8,128)(2,1)}, u32[]{:S(2)}) copy-start(bf16[1,1024,768]{2,1,0:T(8,128)(2,1)} %param.19) | copy-start | bytes 4718596
  456.0 63.6 %collective-permute-start = (bf16[1024,768]{1,0:T(8,128)(2,1)}, bf16[1024,768]{1,0:T(8,128)(2,1)}, u32[]{:S(2)}, u32[]{:S(2)}) collective-permute-start(bf16[1024,768]{1,0:T(8,128)(2,1)} %add_convert_fusion.1), channel_id=1, source_target_pairs={{0,1},{1,0},{2,3},{3,2},{4,5},{5,4},{6,7},{7,6},{8,9},{9,8},{10,11... | collective-permute-start | bytes 4718600 | tf_op jit(solution)/shard_map/ppermute | solution.py:204
  487.6 32.0 %copy-start.11 = (f32[768]{0:T(1024)S(1)}, f32[768]{0:T(1024)}, u32[]{:S(2)}) copy-start(f32[768]{0:T(1024)} %param.36) | copy-start | bytes 9220
  487.6 32.0 %copy-start.12 = (f32[768]{0:T(1024)S(1)}, f32[768]{0:T(1024)}, u32[]{:S(2)}) copy-start(f32[768]{0:T(1024)} %param.32) | copy-start | bytes 9220
  612.7 8.4 %copy-start.10 = (f32[768]{0:T(1024)}, f32[768]{0:T(1024)S(1)}, u32[]{:S(2)}) copy-start(f32[768]{0:T(1024)S(1)} %split.43) | copy-start | bytes 9220
  614.5 3.3 copy-start.5
Sparse Core Ops, SparseCore 0:
  10.2 23.4 all-gather.8
  35.8 40.7 all-gather.10
  78.8 115.3 all-gather.12
  310.7 58.4 reduce-scatter.4
  371.4 60.2 reduce-scatter.6
  434.1 47.8 reduce-scatter.10
  484.6 33.0 reduce-scatter.8
  520.2 90.2 all-reduce.2

commit v2 on v1

--- a/solution.py
+++ b/solution.py
@@ -60,14 +60,12 @@
     grad_ref,
     mixed_ref,
     grad_query_ref,
-    grad_key_ref,
-    grad_value_ref,
+    grad_pair_ref,
     key_rows,
     value_rows,
     key_sum,
     value_sum,
     score_buf,
-    prob_buf,
 ):
     chunks, chunk_len, query_len = score_buf.shape
     block = pl.program_id(2)
@@ -105,7 +103,7 @@
         total, mixed = carry
         probs = jnp.exp(score_buf[c] - row_max)
         low = probs.astype(jnp.bfloat16)
-        prob_buf[c] = low
+        score_buf[c] = probs
         mixed = mixed + jnp.dot(value_ref[c], low, preferred_element_type=jnp.float32)
         return total + fold_rows(probs, jnp.sum), mixed
 
@@ -126,9 +124,10 @@
     grad_back = (grad.astype(jnp.float32) * inverse).T.astype(jnp.bfloat16)
 
     def back_step(c, grad_query):
-        low = prob_buf[c]
+        probs = score_buf[c]
+        low = probs.astype(jnp.bfloat16)
         grad_probs = jnp.dot(value_rows[c], grad, preferred_element_type=jnp.float32)
-        grad_scores = (low.astype(jnp.float32) * (grad_probs - delta)).astype(jnp.bfloat16)
+        grad_scores = (probs * (grad_probs - delta)).astype(jnp.bfloat16)
         value_sum[c] += jnp.dot(low, grad_back, preferred_element_type=jnp.float32)
         key_sum[c] += jnp.dot(grad_scores, query_back, preferred_element_type=jnp.float32)
         return grad_query + jnp.dot(
@@ -143,8 +142,8 @@
     @pl.when(block == pl.num_programs(2) - 1)
     def _():
         def turn(c, carry):
-            grad_key_ref[c] = key_sum[c].T.astype(jnp.bfloat16)
-            grad_value_ref[c] = value_sum[c].T.astype(jnp.bfloat16)
+            grad_pair_ref[c, 0] = key_sum[c].T.astype(jnp.bfloat16)
+            grad_pair_ref[c, 1] = value_sum[c].T.astype(jnp.bfloat16)
             return carry
 
         lax.fori_loop(0, chunks, turn, 0)
@@ -174,12 +173,15 @@
             pl.BlockSpec((chunks, HEAD_DIM, block_len), lambda s, h, i: (0, h + heads, s)),
             one,
         ],
-        out_specs=[one, one, every, every],
+        out_specs=[
+            one,
+            one,
+            pl.BlockSpec((chunks, 2, HEAD_DIM, block_len), lambda s, h, i: (0, 0, h, s)),
+        ],
         out_shape=[
             jax.ShapeDtypeStruct((width, row_count), jnp.bfloat16),
             jax.ShapeDtypeStruct((width, row_count), jnp.float32),
-            jax.ShapeDtypeStruct((chunks, width, row_count), jnp.bfloat16),
-            jax.ShapeDtypeStruct((chunks, width, row_count), jnp.bfloat16),
+            jax.ShapeDtypeStruct((chunks, 2, width, row_count), jnp.bfloat16),
         ],
         scratch_shapes=[
             pltpu.VMEM((chunks, block_len, HEAD_DIM), jnp.bfloat16),
@@ -187,7 +189,6 @@
             pltpu.VMEM((chunks, block_len, HEAD_DIM), jnp.float32),
             pltpu.VMEM((chunks, block_len, HEAD_DIM), jnp.float32),
             pltpu.VMEM((chunks, block_len, query_len), jnp.float32),
-            pltpu.VMEM((chunks, block_len, query_len), jnp.bfloat16),
         ],
         compiler_params=pltpu.CompilerParams(vmem_limit_bytes=50 * 2**20),
         cost_estimate=pl.CostEstimate(
@@ -205,9 +206,65 @@
     return low.astype(jnp.float32) + other.astype(jnp.float32)
 
 
-def owner_sum(grads):
-    own = lax.psum_scatter(grads.astype(jnp.bfloat16), "dp", scatter_dimension=0, tiled=True)
-    return lax.psum(own, "context").astype(jnp.float32)
+def gather_rows(shard):
+    count = lax.axis_size("dp")
+    chips = count // 2
+    here = lax.axis_index("dp")
+    parts = [shard] + [
+        lax.ppermute(shard, "dp", [(i, (i + 2 * step) % count) for i in range(count)])
+        for step in range(1, chips)
+    ]
+    parts = jnp.stack(parts)
+    other = lax.ppermute(parts, "dp", [(i, i ^ 1) for i in range(count)])
+    first = here % 2 == 0
+    even = jnp.where(first, parts, other)
+    odd = jnp.where(first, other, parts)
+    both = jnp.stack([even, odd], axis=1)
+    ordered = [
+        lax.dynamic_index_in_dim(both, (here // 2 - chip) % chips, 0, keepdims=False)
+        for chip in range(chips)
+    ]
+    return jnp.stack(ordered).reshape(count * shard.shape[0], shard.shape[1])
+
+
+def scatter_core(grads):
+    count = lax.axis_size("dp")
+    core = lax.axis_index("dp") % 2
+    split = grads.astype(jnp.bfloat16).reshape(count // 2, 2, -1, grads.shape[1])
+    keep = lax.dynamic_index_in_dim(split, core, 1, keepdims=False)
+    send = lax.dynamic_index_in_dim(split, 1 - core, 1, keepdims=False)
+    other = lax.ppermute(send, "dp", [(i, i ^ 1) for i in range(count)])
+    return (keep.astype(jnp.float32) + other.astype(jnp.float32)).astype(jnp.bfloat16)
+
+
+def scatter_chips(half):
+    count = lax.axis_size("dp")
+    chips = count // 2
+    chip = lax.axis_index("dp") // 2
+    total = lax.dynamic_index_in_dim(half, chip, 0, keepdims=False).astype(jnp.float32)
+    for step in range(1, chips):
+        send = lax.dynamic_index_in_dim(half, (chip + step) % chips, 0, keepdims=False)
+        other = lax.ppermute(
+            send, "dp", [(i, (i + 2 * step) % count) for i in range(count)]
+        )
+        total = total + other.astype(jnp.float32)
+    return total.astype(jnp.bfloat16)
+
+
+def small_sum(vector, axis):
+    count = lax.axis_size(axis)
+    here = lax.axis_index(axis)
+    parts = [vector] + [
+        lax.ppermute(vector, axis, [(i, (i + step) % count) for i in range(count)])
+        for step in range(1, count)
+    ]
+    parts = jnp.stack(parts)
+    total = lax.dynamic_index_in_dim(parts, here % count, 0, keepdims=False)
+    for owner in range(1, count):
+        total = total + lax.dynamic_index_in_dim(
+            parts, (here - owner) % count, 0, keepdims=False
+        )
+    return total
 
 
 def body(
@@ -244,16 +301,18 @@
     def mm(spec, left, right):
         return jnp.einsum(spec, left, right, preferred_element_type=f32)
 
-    full_qkv = lax.all_gather(
-        jnp.concatenate([w_query, w_key, w_value], axis=1), "dp", axis=0, tiled=True
-    )
+    groups = 2 if (part_width // HEAD_DIM) % 2 == 0 else 1
+    group_width = part_width // groups
+
     places = lax.all_gather(positions, "context", axis=0, tiled=False)
-    full_rest = lax.all_gather(
-        jnp.concatenate([w_up, w_down.T, w_out.T], axis=1), "dp", axis=0, tiled=True
-    )
+    full_first = gather_rows(jnp.concatenate([w_query, w_key, w_value, w_out.T], axis=1))
+    rest = jnp.concatenate([w_up, w_down.T], axis=1)
+    full_first, places, rest = lax.optimization_barrier((full_first, places, rest))
+    full_qkv = full_first[:, : 3 * part_width]
+    full_out = full_first[:, 3 * part_width :]
+    full_rest = gather_rows(rest)
     full_up = full_rest[:, :ff_part]
-    full_down = full_rest[:, ff_part : 2 * ff_part]
-    full_out = full_rest[:, 2 * ff_part :]
+    full_down = full_rest[:, ff_part:]
 
     plain, inv_std = normalize(flat_in)
     normed_one = (plain * first_gain + first_shift).astype(low)
@@ -267,9 +326,13 @@
     query = rotate_rows(qkv[:part_width], cosine, sine).astype(low)
     key = rotate_rows(qkv[part_width : 2 * part_width], cosine, sine).astype(low)
     value = qkv[2 * part_width :].astype(low)
-    key_value = lax.all_gather(
-        jnp.concatenate([key, value], axis=0), "context", axis=0, tiled=False
-    )
+    spans = [slice(g * group_width, (g + 1) * group_width) for g in range(groups)]
+    key_values = []
+    for span in spans:
+        pair = jnp.concatenate([key[span], value[span]], axis=0)
+        if key_values:
+            pair, key_values[-1] = lax.optimization_barrier((pair, key_values[-1]))
+        key_values.append(lax.all_gather(pair, "context", axis=0, tiled=False))
 
     grad_mixed = mm("dc,rd->cr", full_out, upstream).astype(low)
     inner = mm("rd,df->rf", normed_two, full_up) + up_bias
@@ -280,18 +343,35 @@
     grad_ff = jnp.concatenate(
         [mm("rd,rf->df", normed_two, grad_inner), mm("rd,rf->df", upstream, hidden)], axis=1
     )
-    own_ff = owner_sum(grad_ff)
+    half_ff = scatter_core(grad_ff)
     back_two = mm("rf,df->rd", grad_inner, full_up)
     out_two = mm("rf,df->rd", hidden, full_down)
     upstream_wide = upstream.astype(f32)
 
-    mixed, grad_query_rot, grad_key_all, grad_value_all = attend(
-        query, key_value, grad_mixed, positions, places, seq_count, block_len
-    )
-    key_part = lax.psum_scatter(grad_key_all, "context", scatter_dimension=0, tiled=False)
-    value_part = lax.psum_scatter(grad_value_all, "context", scatter_dimension=0, tiled=False)
-
+    query, grad_mixed, half_ff, back_two, out_two = lax.optimization_barrier(
+        (query, grad_mixed, half_ff, back_two, out_two)
+    )
+    quarter_ff = scatter_chips(half_ff)
+    mixed, grad_query_rot, key_parts, value_parts = [], [], [], []
+    for span, key_value in zip(spans, key_values):
+        mixed_part, query_part, pair_all = attend(
+            query[span], key_value, grad_mixed[span], positions, places, seq_count, block_len
+        )
+        pair = lax.psum_scatter(pair_all, "context", scatter_dimension=0, tiled=False)
+        mixed.append(mixed_part)
+        grad_query_rot.append(query_part)
+        key_parts.append(pair[0])
+        value_parts.append(pair[1])
+    mixed = jnp.concatenate(mixed, axis=0)
+    grad_query_rot = jnp.concatenate(grad_query_rot, axis=0)
     summed = over_tensor(mm("cr,dc->rd", mixed, full_out) + out_two)
+    grad_out = mm("rd,cr->dc", upstream, mixed)
+    quarter_ff, summed, grad_out, value_parts[-1], key_parts[-1] = lax.optimization_barrier(
+        (quarter_ff, summed, grad_out, value_parts[-1], key_parts[-1])
+    )
+    key_part = jnp.concatenate(key_parts, axis=0)
+    value_part = jnp.concatenate(value_parts, axis=0)
+    own_ff = lax.psum(quarter_ff, "context")
     block_out = (
         (flat_in + summed + out_bias + down_bias)
         .astype(low)
@@ -315,9 +395,13 @@
     ).reshape(seq_count, block_len, model_width)
 
     grad_late = jnp.concatenate(
-        [mm("rd,cr->dc", upstream, mixed), mm("rd,cr->dc", normed_one, grad_qkv)], axis=1
-    )
-    own_late = owner_sum(grad_late)
+        [grad_out, mm("rd,cr->dc", normed_one, grad_qkv)], axis=1
+    )
+    quarter_late, own_ff = lax.optimization_barrier(
+        (scatter_chips(scatter_core(grad_late)), own_ff)
+    )
+    own_late = lax.psum(quarter_late, "context").astype(f32)
+    own_ff = own_ff.astype(f32)
 
     gains = jnp.stack(
         [
@@ -334,20 +418,11 @@
             jnp.sum(upstream_wide, axis=0),
         ]
     )
-    vectors = lax.all_gather(
-        jnp.concatenate([gains, biases]), ("tensor", "dp", "context"), axis=0, tiled=False
-    )
-    sum_g1, sum_s1, sum_g2, sum_s2 = jnp.sum(vectors[:, : gains.shape[0]], axis=0).reshape(
-        4, model_width
-    )
-    sides = lax.axis_size("tensor")
-    own_side = lax.dynamic_index_in_dim(
-        vectors[:, gains.shape[0] :].reshape(sides, -1, biases.shape[0]),
-        lax.axis_index("tensor"),
-        0,
-        keepdims=False,
-    )
-    sum_b = jnp.sum(own_side, axis=0)
+    vector = jnp.concatenate([gains, biases]).reshape(1, -1)
+    vector = small_sum(small_sum(vector, "dp"), "context")
+    sum_g = small_sum(vector[:, : gains.shape[0]], "tensor").reshape(4, model_width)
+    sum_g1, sum_s1, sum_g2, sum_s2 = sum_g
+    sum_b = vector[0, gains.shape[0] :]
     cuts = [part_width, 2 * part_width, 3 * part_width, 3 * part_width + ff_part]
     sum_qb, sum_kb, sum_vb, sum_ub, sum_ob = jnp.split(sum_b, cuts)
     shard_out, shard_query, shard_key, shard_value = jnp.split(own_late, 4, axis=1)

time: 629 us -> 484 us (0.77)
  waiting for transfers between devices: 305 us -> 181 us
  blocking collectives: 100 us -> 14.2 us
  other arithmetic: 28.4 us -> 52.1 us
  local copies, waits for them, and re-layouts: 16.4 us -> 34.1 us
  starting transfers between devices: 2.76 us -> 20.4 us
    all_gather x3 -> x2, waiting for transfers between devices: 158 us -> 28.8 us  [body(): key_values.append(lax.all_gather(pair, 'context', axis=0, tiled=False))]
    reduce_scatter x4 -> x2, waiting for transfers between devices: 115 us -> 13.7 us  [body(): lax.psum_scatter(pair_all, 'context', scatter_dimension=0, tiled=False)]
    all_gather x1 -> x0, blocking collectives: 87.1 us -> none  [body(): lax.all_gather(jnp.concatenate([gains, biases]), ('tensor', 'dp', 'contex...]
    ppermute x0 -> x15, waiting for transfers between devices: none -> 68.8 us  [the longest x2 34.3 us: gather_rows(): lax.ppermute(shard, 'dp', [(i, (i + 2 * step) % count) for i in range(cou...]
    psum x1 -> x2, waiting for transfers between devices: 0.01 us -> 33.7 us  [the longest x1 33.7 us: body(): own_late = lax.psum(quarter_late, 'context').astype(f32)]
    ppermute x0 -> x15, starting transfers between devices: none -> 16.4 us  [the longest x7 7.95 us: small_sum(): lax.ppermute(vector, axis, [(i, (i + step) % count) for i in range(count)])]
    another operation x2 -> x13, other arithmetic: 0.2 us -> 14 us  [the longest x4 4.4 us: gather_rows(): both = jnp.stack([even, odd], axis=1)]
    convert_element_type x2 -> x7, other arithmetic: 1.43 us -> 10.4 us  [the longest x2 4.42 us: scatter_core(): (keep.astype(jnp.float32) + other.astype(jnp.float32)).astype(jnp.bfloat16)]
  transfers between devices with their start and end apart: 10 -> 23, of which waited for: 8 -> 12; matrix products, arithmetic and copies ran while one was open for 12% -> 22% of each run, Pallas kernels for 0% -> 24%
where the time goes in v2:
time: 484 us; the launch traced here: 477 us
  waiting for transfers between devices  181 us (37%)
  Pallas kernels  113 us (23%)
  other arithmetic  52.1 us (11%)
  matrix products  47.2 us (10%)
  local copies, waits for them, and re-layouts  34.1 us (7%)
  starting transfers between devices  20.4 us (4%)
  between operations  15.5 us (3%)
  blocking collectives  14.2 us (3%)
    pallas_call x2, Pallas kernels, attend(): pl.pallas_call(attend_kernel, grid=(seq_count, heads, blocks), in_specs=[...  113 us
    dot_general x12, matrix products, mm(): return jnp.einsum(spec, left, right, preferred_element_type=f32)  47.2 us
    ppermute x2, waiting for transfers between devices, over_tensor(): other = lax.ppermute(low, 'tensor', [(0, 1), (1, 0)])  36.1 us
    ppermute x2, waiting for transfers between devices, gather_rows(): lax.ppermute(shard, 'dp', [(i, (i + 2 * step) % count) for i in range(cou...  34.3 us
    psum x1, waiting for transfers between devices, body(): own_late = lax.psum(quarter_late, 'context').astype(f32)  33.7 us
    ppermute x2, waiting for transfers between devices, scatter_chips(): lax.ppermute(send, 'dp', [(i, (i + 2 * step) % count) for i in range(coun...  29.3 us
    all_gather x2, waiting for transfers between devices, body(): key_values.append(lax.all_gather(pair, 'context', axis=0, tiled=False))  28.8 us
    all_gather x1, blocking collectives, body(): places = lax.all_gather(positions, 'context', axis=0, tiled=False)  14.2 us
  transfers between devices with their start and end apart: 23, of which 12 were waited for; matrix products, arithmetic and copies ran while one was open for 22% of the time, Pallas kernels for 24%

profile of v2, /device:TPU:0, one launch (start us, length us, event | category | flops | bytes accessed | tf_op | source)
XLA Modules:
  0.0 477.4 jit_solution(13430067657062345730)
XLA Ops:
  7.3 1.3 fusion.78
  8.5 3.0 collective-permute-start
  11.5 13.3 %collective-permute-done = bf16[192,1536]{1,0:T(8,128)(2,1)S(1)} collective-permute-done((bf16[192,1536]{1,0:T(8,128)(2,1)S(1)}, bf16[192,1536]{1,0:T(8,128)(2,1)S(1)}, u32[]{:S(2)}, u32[]{:S(2)}) %collective-permute-start) | collective-permute-done | bytes 589856 | tf_op jit(solution)/shard_map/ppermute | solution.py:214
  24.8 1.1 pad_maximum_fusion.5
  26.0 14.2 %all-gather.3 = s32[4,1,1024]{2,1,0:T(1,128)} all-gather(s32[1,1,1024]{2,1,0:T(1,128)S(1)} %bitcast.205), channel_id=2, replica_groups=mesh['dp'=4,'context'=4,'tensor'=2] {'context'}, dimensions={0}, use_global_device_ids=true | all-gather | bytes 20480 | tf_op jit(solution)/shard_map/all_gather | solution.py:307
  40.1 1.2 pad_maximum_fusion.6
  41.4 1.4 select_bitcast_fusion.2
  43.0 1.6 pad_maximum_fusion.1
  44.6 1.5 collective-permute-start.2
  47.0 1.8 fusion.80
  48.8 21.0 %collective-permute-done.2 = bf16[192,3072]{1,0:T(8,128)(2,1)S(1)} collective-permute-done((bf16[192,3072]{1,0:T(8,128)(2,1)S(1)}, bf16[192,3072]{1,0:T(8,128)(2,1)S(1)}, u32[]{:S(2)}, u32[]{:S(2)}) %collective-permute-start.2) | collective-permute-done | bytes 1179680 | tf_op jit(solution)/shard_map/ppermute | solution.py:214
  69.8 1.7 pad_maximum_fusion.2
  71.7 2.6 copy.46
  75.2 4.3 fusion.89
  82.3 2.3 select_bitcast_fusion
  85.8 3.3 multiply_convert_fusion
  89.1 2.9 convolution_convert_fusion
  92.0 6.3 %convert_reduce_fusion = (f32[1536]{0:T(1024)}, bf16[1024,1536]{1,0:T(8,128)(2,1)S(1)}) fusion(f32[1024,1536]{1,0:T(8,128)S(1)} %get-tuple-element.130, f32[1536]{0:T(1024)S(1)} %copy-done.56, bf16[768,3072]{1,0:T(8,128)(2,1)S(1)} %bitcast.219, bf16[1,1024,768]{2,1,0:T(8,128)(2,1)S(1)} %copy-done.29), kind=kOutput, calls=%fused_computation.7 | convolution fusion | flops 2436364800 | bytes 13383680 | tf_op jit(solution)/shard_map/rd,df->rf/dot_general | solution.py:302
  98.2 2.8 convolution_convert_fusion.1
  101.1 2.0 fusion.34
  103.7 2.2 slice.237
  107.4 1.3 pad_maximum_fusion.7
  108.8 3.3 fusion.59
  112.1 6.0 %fusion.42 = f32[1024,768]{1,0:T(8,128)} fusion(bf16[1024,1536]{1,0:T(8,128)(2,1)S(1)} %copy-done.59, bf16[768,3072]{1,0:T(8,128)(2,1)} %bitcast.220), kind=kOutput, calls=%fused_computation.84 | convolution fusion | flops 2415919104 | bytes 8650752 | tf_op jit(solution)/shard_map/rf,df->rd/dot_general | solution.py:302
  118.0 28.8 %all-gather.7.cloned.1.call-done = bf16[1536,1024]{1,0:T(8,128)(2,1)} async-done(((bf16[384,1024]{1,0:T(8,128)(2,1)}), bf16[1536,1024]{1,0:T(8,128)(2,1)}) %all-gather.7.cloned.1.call-update) | async-done | bytes 3145744 | tf_op jit(solution)/shard_map/all_gather | solution.py:335
  147.1 7.1 %fusion.46 = f32[1024,768]{1,0:T(8,128)} fusion(bf16[1024,1536]{1,0:T(8,128)(2,1)} %copy-done.57, bf16[768,3072]{1,0:T(8,128)(2,1)} %bitcast.221), kind=kOutput, calls=%fused_computation.88 | convolution fusion | flops 2415919104 | bytes 8650752 | tf_op jit(solution)/shard_map/rf,df->rd/dot_general | solution.py:302
  154.3 4.1 fusion.6
  159.9 56.4 %shard_map.322 = (bf16[192,1024]{1,0:T(8,128)(2,1)S(1)}, f32[192,1024]{1,0:T(8,128)S(1)}, bf16[4,2,192,1024]{3,2,1,0:T(8,128)(2,1)}) custom-call(s32[2,1,512]{2,1,0:T(1,128)S(1)} %bitcast.206, s32[4,1024,128]{2,1,0:T(8,128)S(1)} %broadcast_in_dim.5.key_places, bf16[192,1024]{1,0:T(8,128)(2,1)S(1)} %get-tuple-element.137.query_ref, ...), custom_call_target="tpu_custom_call" | custom-call | flops 38654705664 | bytes 33554432 | tf_op jit(solution)/shard_map/pallas_call | solution.py:165
  218.1 56.4 %shard_map.323 = (bf16[192,1024]{1,0:T(8,128)(2,1)S(1)}, f32[192,1024]{1,0:T(8,128)S(1)}, bf16[4,2,192,1024]{3,2,1,0:T(8,128)(2,1)}) custom-call(s32[2,1,512]{2,1,0:T(1,128)S(1)} %bitcast.207, s32[4,1024,128]{2,1,0:T(8,128)S(1)} %broadcast_in_dim.5.key_places, bf16[192,1024]{1,0:T(8,128)(2,1)S(1)} %copy-done.2, bf16[4,384,1024]{2,1,0:T(8,128)(2,1)} %bitcast.255, ...), custom_call_target="tpu_custom_call" | custom-call | flops 38654705664 | bytes 33554432 | tf_op jit(solution)/shard_map/pallas_call | solution.py:165
  276.5 2.4 dynamic-slice_bitcast_fusion
  278.9 1.4 collective-permute-start.5
  281.3 2.2 fusion.72
  284.1 1.6 collective-permute-start.6
  285.6 21.2 %collective-permute-done.5 = bf16[192,3072]{1,0:T(8,128)(2,1)} collective-permute-done((bf16[192,3072]{1,0:T(8,128)(2,1)}, bf16[192,3072]{1,0:T(8,128)(2,1)}, u32[]{:S(2)}, u32[]{:S(2)}) %collective-permute-start.5) | collective-permute-done | bytes 1179680 | tf_op jit(solution)/shard_map/ppermute | solution.py:247
  306.9 3.0 fusion.41
  310.1 1.2 copy-done.28
  312.1 1.6 fusion.62
  313.8 6.3 %collective-permute-done.6 = bf16[1024,768]{1,0:T(8,128)(2,1)} collective-permute-done((bf16[1024,768]{1,0:T(8,128)(2,1)S(1)}, bf16[1024,768]{1,0:T(8,128)(2,1)}, u32[]{:S(2)}, u32[]{:S(2)}) %collective-permute-start.6) | collective-permute-done | bytes 1572896 | tf_op jit(solution)/shard_map/ppermute | solution.py:205
  320.0 3.5 convert_add_fusion.3
  323.6 1.2 slice_bitcast_fusion.2
  324.7 13.7 %reduce-scatter.3.cloned.1.call-done = bf16[1,2,192,1024]{3,2,1,0:T(8,128)(2,1)} async-done(((bf16[4,2,192,1024]{3,2,1,0:T(8,128)(2,1)}), bf16[1,2,192,1024]{3,2,1,0:T(8,128)(2,1)}) %reduce-scatter.3.cloned.1.call-update) | async-done | bytes 786448 | tf_op jit(solution)/shard_map/reduce_scatter | solution.py:360
  338.4 1.2 slice_bitcast_fusion.3
  340.5 1.5 subtract_convert_fusion.1
  342.6 3.7 add_convert_fusion
  346.3 1.5 collective-permute-start.7
  347.8 2.2 copy.48
  350.1 2.5 convert_reduce_fusion.1
  352.6 29.8 %collective-permute-done.7 = bf16[1024,768]{1,0:T(8,128)(2,1)} collective-permute-done((bf16[1024,768]{1,0:T(8,128)(2,1)S(1)}, bf16[1024,768]{1,0:T(8,128)(2,1)}, u32[]{:S(2)}, u32[]{:S(2)}) %collective-permute-start.7) | collective-permute-done | bytes 1572896 | tf_op jit(solution)/shard_map/ppermute | solution.py:205
  382.4 4.5 fusion.32
  388.2 5.9 %fusion.81 = (bf16[768,1024]{0,1:T(8,128)(2,1)S(1)}, f32[1,1024,768]{2,1,0:T(8,128)}, f32[768]{0:T(1024)S(1)}, bf16[1,1024,768]{2,1,0:T(8,128)(2,1)}) fusion(f32[768]{0:T(1024)} %param.22, f32[768]{0:T(1024)} %param.21, f32[1024]{0:T(1024)S(1)} %add_rsqrt_fusion, f32[1024]{0:T(1024)S(1)} %broadcast_multiply_fusion.2, ...), kind=kLoop, calls=%fused_computation.183 | loop fusion | flops 15727872 | bytes 15760384 | tf_op jit(solution)/shard_map/rd,cr->dc/dot_general | solution.py:302
  395.4 1.5 collective-permute-start.9
  397.1 1.6 copy.49
  398.8 3.8 convolution_convert_fusion.2
  404.8 2.5 collective-permute-start.13
  407.6 1.9 collective-permute-start.11
  409.6 2.7 collective-permute-done.12
  413.8 1.5 collective-permute-start.16
  415.9 1.5 collective-permute-start.14
  418.0 1.5 collective-permute-done.14
  419.6 8.1 %collective-permute-done.16 = bf16[192,1536]{1,0:T(8,128)(2,1)S(1)} collective-permute-done((bf16[192,1536]{1,0:T(8,128)(2,1)S(1)}, bf16[192,1536]{1,0:T(8,128)(2,1)S(1)}, u32[]{:S(2)}, u32[]{:S(2)}) %collective-permute-start.16) | collective-permute-done | bytes 589856 | tf_op jit(solution)/shard_map/ppermute | solution.py:247
  429.4 2.2 slice.192
  431.8 1.1 slice_bitcast_fusion
  433.0 33.7 %all-reduce.5.cloned.1.call-done = bf16[192,1536]{1,0:T(8,128)(2,1)} async-done(((bf16[192,1536]{1,0:T(8,128)(2,1)}), bf16[192,1536]{1,0:T(8,128)(2,1)}) %all-reduce.5.cloned.1.call-update) | async-done | bytes 589840 | tf_op jit(solution)/shard_map/psum | solution.py:403
  466.6 1.3 convert_element_type.173
  (212 shorter events, 29.9 us)
Async XLA Ops:
  7.2 18.8 %copy-start.7 = (s32[1,1024]{1,0:T(1,128)S(1)}, s32[1,1024]{1,0:T(1,128)}, u32[]{:S(2)}) copy-start(s32[1,1024]{1,0:T(1,128)} %param.20) | copy-start | bytes 12292
  7.2 32.9 %copy-start.34 = (bf16[1536,192]{0,1:T(8,128)(2,1)S(1)}, bf16[1536,192]{0,1:T(8,128)(2,1)}, u32[]{:S(2)}) copy-start(bf16[1536,192]{0,1:T(8,128)(2,1)} %param.35) | copy-start | bytes 1769476
  7.2 139.6 %all-gather.7.cloned.1.call-start = ((), (), s32[]{:S(2)}) async-start(), calls=%async_computation.6 | async-start | bytes 3932160 | tf_op jit(solution)/shard_map/all_gather | solution.py:335
  8.5 16.3 %collective-permute-start = (bf16[192,1536]{1,0:T(8,128)(2,1)S(1)}, bf16[192,1536]{1,0:T(8,128)(2,1)S(1)}, u32[]{:S(2)}, u32[]{:S(2)}) collective-permute-start(bf16[192,1536]{1,0:T(8,128)(2,1)S(1)} %get-tuple-element.119), channel_id=1, source_target_pairs={{0,16},{8,24},{16,0},{24,8},{1,17},{9,25},{17,1},{25,9},{2,18},{10... | collective-permute-start | bytes 1769480 | tf_op jit(solution)/shard_map/ppermute | solution.py:214
  26.0 15.4 %collective-permute-start.1 = (bf16[2,192,1536]{2,1,0:T(8,128)(2,1)}, bf16[2,192,1536]{2,1,0:T(8,128)(2,1)}, u32[]{:S(2)}, u32[]{:S(2)}) collective-permute-start(bf16[2,192,1536]{2,1,0:T(8,128)(2,1)} %pad_maximum_fusion.5), channel_id=1, source_target_pairs={{0,8},{8,0},{16,24},{24,16},{1,9},{9,1},{17,25},{25,17},{2,10},{10... | collective-permute-start | bytes 3538952 | tf_op jit(solution)/shard_map/ppermute | solution.py:218
  43.0 3.1 copy-start.8
  44.6 2.4 copy-start.46
  44.6 2.4 copy-start.47
  44.6 25.2 %collective-permute-start.2 = (bf16[192,3072]{1,0:T(8,128)(2,1)S(1)}, bf16[192,3072]{1,0:T(8,128)(2,1)S(1)}, u32[]{:S(2)}, u32[]{:S(2)}) collective-permute-start(bf16[192,3072]{1,0:T(8,128)(2,1)S(1)} %pad_maximum_fusion.6), channel_id=1, source_target_pairs={{0,16},{8,24},{16,0},{24,8},{1,17},{9,25},{17,1},{25,9},{2,18},{10... | collective-permute-start | bytes 3538952 | tf_op jit(solution)/shard_map/ppermute | solution.py:214
  71.6 2.8 copy-start.53
  71.6 2.8 copy-start.54
  71.6 2.8 copy-start.55
  71.6 3.6 copy-start.50
  71.6 3.6 copy-start.51
  71.6 10.6 %collective-permute-start.3 = (bf16[2,192,3072]{2,1,0:T(8,128)(2,1)}, bf16[2,192,3072]{2,1,0:T(8,128)(2,1)}, u32[]{:S(2)}, u32[]{:S(2)}) collective-permute-start(bf16[2,192,3072]{2,1,0:T(8,128)(2,1)} %pad_maximum_fusion.2), channel_id=1, source_target_pairs={{0,8},{8,0},{16,24},{24,16},{1,9},{9,1},{17,25},{25,17},{2,10},{10... | collective-permute-start | bytes 7077896 | tf_op jit(solution)/shard_map/ppermute | solution.py:218
  75.2 4.6 copy-start.35
  82.0 135.1 %all-gather.9.cloned.1.call-start = ((), (), s32[]{:S(2)}) async-start(), calls=%async_computation.7 | async-start | bytes 3932160 | tf_op jit(solution)/shard_map/all_gather | solution.py:335
  85.5 6.5 %copy-start.16 = (bf16[2,2,192,3072]{3,2,1,0:T(8,128)(2,1)}, bf16[2,2,192,3072]{3,2,1,0:T(8,128)(2,1)S(1)}, u32[]{:S(2)}) copy-start(bf16[2,2,192,3072]{3,2,1,0:T(8,128)(2,1)S(1)} %pad_maximum_fusion) | copy-start | bytes 14155780
  85.8 3.3 copy-start.29
  89.0 2.9 copy-start.57
  92.0 6.3 %copy-start.31 = (bf16[768,1024]{1,0:T(8,128)(2,1)S(1)}, bf16[768,1024]{1,0:T(8,128)(2,1)}, u32[]{:S(2)}) copy-start(bf16[768,1024]{1,0:T(8,128)(2,1)} %copy.46) | copy-start | bytes 4718596
  98.2 2.8 copy-start.58
  101.1 4.8 %copy-start.41 = (s32[4,1,1024]{2,1,0:T(1,128)S(1)}, s32[4,1,1024]{2,1,0:T(1,128)}, u32[]{:S(2)}) copy-start(s32[4,1,1024]{2,1,0:T(1,128)} %all-gather.3) | copy-start | bytes 49156
  103.3 51.0 %collective-permute-start.4 = (bf16[2,192,3072]{2,1,0:T(8,128)(2,1)}, bf16[2,192,3072]{2,1,0:T(8,128)(2,1)}, u32[]{:S(2)}, u32[]{:S(2)}) collective-permute-start(bf16[2,192,3072]{2,1,0:T(8,128)(2,1)} %fusion.34), channel_id=1, source_target_pairs={{0,8},{8,0},{16,24},{24,16},{1,9},{9,1},{17,25},{25,17},{2,10},{10... | collective-permute-start | bytes 7077896 | tf_op jit(solution)/shard_map/ppermute | solution.py:236
  107.4 4.6 copy-start.59
  146.9 176.7 %reduce-scatter.5.cloned.1.call-start = ((), (), s32[]{:S(2)}) async-start(), calls=%async_computation.3 | async-start | bytes 3932160 | tf_op jit(solution)/shard_map/reduce_scatter | solution.py:360
  147.1 7.1 %copy-start.11 = (bf16[2,2,192,1536]{3,2,1,0:T(8,128)(2,1)S(1)}, bf16[2,2,192,1536]{3,2,1,0:T(8,128)(2,1)}, u32[]{:S(2)}) copy-start(bf16[2,2,192,1536]{3,2,1,0:T(8,128)(2,1)} %copy-done.10) | copy-start | bytes 7077892
  154.3 4.1 copy-start.33
  217.1 121.4 %reduce-scatter.3.cloned.1.call-start = ((), (), s32[]{:S(2)}) async-start(), calls=%async_computation.2 | async-start | bytes 3932160 | tf_op jit(solution)/shard_map/reduce_scatter | solution.py:360
  276.2 4.2 copy-start.4
  276.2 4.2 copy-start.6
  276.2 152.5 %all-reduce.3.cloned.1.call-start = ((), (), s32[]{:S(2)}) async-start(), calls=%async_computation.4 | async-start | bytes 2359296 | tf_op jit(solution)/shard_map/psum | solution.py:374
  278.9 27.9 %collective-permute-start.5 = (bf16[192,3072]{1,0:T(8,128)(2,1)}, bf16[192,3072]{1,0:T(8,128)(2,1)}, u32[]{:S(2)}, u32[]{:S(2)}) collective-permute-start(bf16[192,3072]{1,0:T(8,128)(2,1)} %dynamic-slice_bitcast_fusion), channel_id=1, source_target_pairs={{0,16},{8,24},{16,0},{24,8},{1,17},{9,25},{17,1},{25,9},{2,18},{10... | collective-permute-start | bytes 3538952 | tf_op jit(solution)/shard_map/ppermute | solution.py:247
  284.0 25.9 %copy-start.1 = (f32[192,1024]{1,0:T(8,128)S(1)}, f32[192,1024]{1,0:T(8,128)}, u32[]{:S(2)}) copy-start(f32[192,1024]{1,0:T(8,128)} %copy-done) | copy-start | bytes 2359300
  284.1 36.0 %collective-permute-start.6 = (bf16[1024,768]{1,0:T(8,128)(2,1)S(1)}, bf16[1024,768]{1,0:T(8,128)(2,1)}, u32[]{:S(2)}, u32[]{:S(2)}) collective-permute-start(bf16[1024,768]{1,0:T(8,128)(2,1)S(1)} %add_convert_fusion.1), channel_id=1, source_target_pairs={{0,1},{1,0},{2,3},{3,2},{4,5},{5,4},{6,7},{7,6},{8,9},{9,8},{10,11... | collective-permute-start | bytes 4718600 | tf_op jit(solution)/shard_map/ppermute | solution.py:205
  310.0 3.7 copy-start.17
  339.6 2.5 copy-start.32
  339.7 2.4 copy-start.25
  339.9 2.7 copy-start.19
  339.9 2.7 copy-start.49
  340.0 2.7 copy-start.52
  342.0 4.3 copy-start.21
  342.1 4.2 copy-start.23
  346.3 36.1 %copy-start.12 = (bf16[1024,768]{1,0:T(8,128)(2,1)}, bf16[1024,768]{1,0:T(8,128)(2,1)S(1)}, u32[]{:S(2)}) copy-start(bf16[1024,768]{1,0:T(8,128)(2,1)S(1)} %get-tuple-element.133) | copy-start | bytes 4718596
  346.3 36.1 %collective-permute-start.7 = (bf16[1024,768]{1,0:T(8,128)(2,1)S(1)}, bf16[1024,768]{1,0:T(8,128)(2,1)}, u32[]{:S(2)}, u32[]{:S(2)}) collective-permute-start(bf16[1024,768]{1,0:T(8,128)(2,1)S(1)} %get-tuple-element.133), channel_id=1, source_target_pairs={{0,1},{1,0},{2,3},{3,2},{4,5},{5,4},{6,7},{7,6},{8,9},{9,8},{10,11... | collective-permute-start | bytes 4718600 | tf_op jit(solution)/shard_map/ppermute | solution.py:205
  347.8 34.6 %copy-start.9 = (bf16[1,1024,768]{2,1,0:T(8,128)(2,1)S(1)}, bf16[1,1024,768]{2,1,0:T(8,128)(2,1)}, u32[]{:S(2)}) copy-start(bf16[1,1024,768]{2,1,0:T(8,128)(2,1)} %param.19) | copy-start | bytes 4718596
  350.1 116.5 %all-reduce.5.cloned.1.call-start = ((), (), s32[]{:S(2)}) async-start(), calls=%async_computation.5 | async-start | bytes 1179648 | tf_op jit(solution)/shard_map/psum | solution.py:403
  388.2 5.9 %copy-start.42 = (f32[3072]{0:T(1024)S(1)}, f32[3072]{0:T(1024)}, u32[]{:S(2)}) copy-start(f32[3072]{0:T(1024)} %reshape.331) | copy-start | bytes 36868
  388.2 5.9 %copy-start.43 = (f32[1152]{0:T(1024)S(1)}, f32[1152]{0:T(1024)}, u32[]{:S(2)}) copy-start(f32[1152]{0:T(1024)} %convert_reduce_fusion.1) | copy-start | bytes 13828
  388.2 5.9 %copy-start.45 = (f32[1536]{0:T(1024)S(1)}, f32[1536]{0:T(1024)}, u32[]{:S(2)}) copy-start(f32[1536]{0:T(1024)} %get-tuple-element.135) | copy-start | bytes 18436
  394.1 4.6 copy-start.22
  394.1 4.6 copy-start.24
  395.4 8.4 %collective-permute-start.10 = (f32[1,6528]{1,0:T(1,128)}, f32[1,6528]{1,0:T(1,128)}, u32[]{:S(2)}, u32[]{:S(2)}) collective-permute-start(f32[1,6528]{1,0:T(1,128)} %reshape.332), channel_id=1, source_target_pairs={{0,24},{8,0},{16,8},{24,16},{1,25},{9,1},{17,9},{25,17},{2,26},{10... | collective-permute-start | bytes 78344 | tf_op jit(solution)/shard_map/ppermute | solution.py:258
  395.4 8.4 %collective-permute-start.9 = (f32[1,6528]{1,0:T(1,128)}, f32[1,6528]{1,0:T(1,128)}, u32[]{:S(2)}, u32[]{:S(2)}) collective-permute-start(f32[1,6528]{1,0:T(1,128)} %reshape.332), channel_id=1, source_target_pairs={{0,16},{8,24},{16,0},{24,8},{1,17},{9,25},{17,1},{25,9},{2,18},{10... | collective-permute-start | bytes 78344 | tf_op jit(solution)/shard_map/ppermute | solution.py:258
  396.9 6.9 %collective-permute-start.8 = (f32[1,6528]{1,0:T(1,128)}, f32[1,6528]{1,0:T(1,128)}, u32[]{:S(2)}, u32[]{:S(2)}) collective-permute-start(f32[1,6528]{1,0:T(1,128)} %reshape.332), channel_id=1, source_target_pairs={{0,8},{8,16},{16,24},{24,0},{1,9},{9,17},{17,25},{25,1},{2,10},{10... | collective-permute-start | bytes 78344 | tf_op jit(solution)/shard_map/ppermute | solution.py:258
  398.8 3.8 copy-start.13
  403.3 10.1 %collective-permute-start.15 = (bf16[2,192,1536]{2,1,0:T(8,128)(2,1)S(1)}, bf16[2,192,1536]{2,1,0:T(8,128)(2,1)S(1)}, u32[]{:S(2)}, u32[]{:S(2)}) collective-permute-start(bf16[2,192,1536]{2,1,0:T(8,128)(2,1)S(1)} %fusion.66), channel_id=1, source_target_pairs={{0,8},{8,0},{16,24},{24,16},{1,9},{9,1},{17,25},{25,17},{2,10},{10... | collective-permute-start | bytes 3538952 | tf_op jit(solution)/shard_map/ppermute | solution.py:236
  404.8 4.8 %collective-permute-start.13 = (f32[1,6528]{1,0:T(1,128)S(1)}, f32[1,6528]{1,0:T(1,128)S(1)}, u32[]{:S(2)}, u32[]{:S(2)}) collective-permute-start(f32[1,6528]{1,0:T(1,128)S(1)} %fusion.97), channel_id=1, source_target_pairs={{0,6},{2,0},{4,2},{6,4},{1,7},{3,1},{5,3},{7,5},{8,14},{10,8},{12,... | collective-permute-start | bytes 78344 | tf_op jit(solution)/shard_map/ppermute | solution.py:258
  407.3 5.0 %collective-permute-start.12 = (f32[1,6528]{1,0:T(1,128)S(1)}, f32[1,6528]{1,0:T(1,128)S(1)}, u32[]{:S(2)}, u32[]{:S(2)}) collective-permute-start(f32[1,6528]{1,0:T(1,128)S(1)} %fusion.97), channel_id=1, source_target_pairs={{0,4},{2,6},{4,0},{6,2},{1,5},{3,7},{5,1},{7,3},{8,12},{10,14},{12... | collective-permute-start | bytes 78344 | tf_op jit(solution)/shard_map/ppermute | solution.py:258
  407.6 5.6 %collective-permute-start.11 = (f32[1,6528]{1,0:T(1,128)S(1)}, f32[1,6528]{1,0:T(1,128)S(1)}, u32[]{:S(2)}, u32[]{:S(2)}) collective-permute-start(f32[1,6528]{1,0:T(1,128)S(1)} %fusion.97), channel_id=1, source_target_pairs={{0,2},{2,4},{4,6},{6,0},{1,3},{3,5},{5,7},{7,1},{8,10},{10,12},{12... | collective-permute-start | bytes 78344 | tf_op jit(solution)/shard_map/ppermute | solution.py:258
  413.8 13.9 %collective-permute-start.16 = (bf16[192,1536]{1,0:T(8,128)(2,1)S(1)}, bf16[192,1536]{1,0:T(8,128)(2,1)S(1)}, u32[]{:S(2)}, u32[]{:S(2)}) collective-permute-start(bf16[192,1536]{1,0:T(8,128)(2,1)S(1)} %dynamic-slice_bitcast_fusion.1), channel_id=1, source_target_pairs={{0,16},{8,24},{16,0},{24,8},{1,17},{9,25},{17,1},{25,9},{2,18},{10... | collective-permute-start | bytes 1769480 | tf_op jit(solution)/shard_map/ppermute | solution.py:247
  415.9 3.7 collective-permute-start.14
  418.0 51.5 %copy-start.44 = (f32[768]{0:T(1024)}, f32[768]{0:T(1024)S(1)}, u32[]{:S(2)}) copy-start(f32[768]{0:T(1024)S(1)} %slice_reduce_fusion.1) | copy-start | bytes 9220
  428.7 2.9 copy-start.15
  (19 other events, 22.7 us)
Sparse Core Ops, SparseCore 0:
  82.2 64.6 all-gather.6
  149.0 62.1 all-gather.8
  217.2 58.7 reduce-scatter.4
  278.2 60.2 reduce-scatter.2
  350.2 55.0 all-reduce.2
  428.9 37.7 all-reduce.4

commit v3 on v2

--- a/solution.py
+++ b/solution.py
@@ -103,6 +103,7 @@
         total, mixed = carry
         probs = jnp.exp(score_buf[c] - row_max)
         low = probs.astype(jnp.bfloat16)
+        probs = low.astype(jnp.float32)
         score_buf[c] = probs
         mixed = mixed + jnp.dot(value_ref[c], low, preferred_element_type=jnp.float32)
         return total + fold_rows(probs, jnp.sum), mixed
@@ -206,15 +207,21 @@
     return low.astype(jnp.float32) + other.astype(jnp.float32)
 
 
-def gather_rows(shard):
+def gather_chips(shard):
+    count = lax.axis_size("dp")
+    return jnp.stack(
+        [shard]
+        + [
+            lax.ppermute(shard, "dp", [(i, (i + 2 * step) % count) for i in range(count)])
+            for step in range(1, count // 2)
+        ]
+    )
+
+
+def gather_cores(parts):
     count = lax.axis_size("dp")
     chips = count // 2
     here = lax.axis_index("dp")
-    parts = [shard] + [
-        lax.ppermute(shard, "dp", [(i, (i + 2 * step) % count) for i in range(count)])
-        for step in range(1, chips)
-    ]
-    parts = jnp.stack(parts)
     other = lax.ppermute(parts, "dp", [(i, i ^ 1) for i in range(count)])
     first = here % 2 == 0
     even = jnp.where(first, parts, other)
@@ -224,7 +231,11 @@
         lax.dynamic_index_in_dim(both, (here // 2 - chip) % chips, 0, keepdims=False)
         for chip in range(chips)
     ]
-    return jnp.stack(ordered).reshape(count * shard.shape[0], shard.shape[1])
+    return jnp.stack(ordered).reshape(count * parts.shape[1], parts.shape[2])
+
+
+def after(value, earlier):
+    return lax.optimization_barrier((value, earlier))[0]
 
 
 def scatter_core(grads):
@@ -251,20 +262,27 @@
     return total.astype(jnp.bfloat16)
 
 
-def small_sum(vector, axis):
+def small_gather(vector, axis):
     count = lax.axis_size(axis)
     here = lax.axis_index(axis)
-    parts = [vector] + [
-        lax.ppermute(vector, axis, [(i, (i + step) % count) for i in range(count)])
-        for step in range(1, count)
+    parts = jnp.stack(
+        [vector]
+        + [
+            lax.ppermute(vector, axis, [(i, (i + step) % count) for i in range(count)])
+            for step in range(1, count)
+        ]
+    )
+    return [
+        lax.dynamic_index_in_dim(parts, (here - owner) % count, 0, keepdims=False)
+        for owner in range(count)
     ]
-    parts = jnp.stack(parts)
-    total = lax.dynamic_index_in_dim(parts, here % count, 0, keepdims=False)
-    for owner in range(1, count):
-        total = total + lax.dynamic_index_in_dim(
-            parts, (here - owner) % count, 0, keepdims=False
-        )
-    return total
+
+
+def small_sum(vector, axis):
+    first, *others = small_gather(vector, axis)
+    for other in others:
+        first = first + other
+    return first
 
 
 def body(
@@ -304,16 +322,13 @@
     groups = 2 if (part_width // HEAD_DIM) % 2 == 0 else 1
     group_width = part_width // groups
 
-    places = lax.all_gather(positions, "context", axis=0, tiled=False)
-    full_first = gather_rows(jnp.concatenate([w_query, w_key, w_value, w_out.T], axis=1))
-    rest = jnp.concatenate([w_up, w_down.T], axis=1)
-    full_first, places, rest = lax.optimization_barrier((full_first, places, rest))
+    first_chips = gather_chips(jnp.concatenate([w_query, w_key, w_value, w_out.T], axis=1))
+    rest = after(jnp.concatenate([w_up, w_down.T], axis=1), first_chips)
+    rest_chips = gather_chips(rest)
+    full_first = gather_cores(first_chips)
+    places = jnp.stack(small_gather(after(positions, first_chips), "context"))
     full_qkv = full_first[:, : 3 * part_width]
     full_out = full_first[:, 3 * part_width :]
-    full_rest = gather_rows(rest)
-    full_up = full_rest[:, :ff_part]
-    full_down = full_rest[:, ff_part:]
-
     plain, inv_std = normalize(flat_in)
     normed_one = (plain * first_gain + first_shift).astype(low)
     normed_two = (plain * second_gain + second_shift).astype(low)
@@ -327,12 +342,14 @@
     key = rotate_rows(qkv[part_width : 2 * part_width], cosine, sine).astype(low)
     value = qkv[2 * part_width :].astype(low)
     spans = [slice(g * group_width, (g + 1) * group_width) for g in range(groups)]
-    key_values = []
-    for span in spans:
-        pair = jnp.concatenate([key[span], value[span]], axis=0)
-        if key_values:
-            pair, key_values[-1] = lax.optimization_barrier((pair, key_values[-1]))
+    pairs = [jnp.concatenate([key[span], value[span]], axis=0) for span in spans]
+    key_values = [lax.all_gather(pairs[0], "context", axis=0, tiled=False)]
+    for pair in pairs[1:]:
+        pair, key_values[-1] = lax.optimization_barrier((pair, key_values[-1]))
         key_values.append(lax.all_gather(pair, "context", axis=0, tiled=False))
+    full_rest = gather_cores(after(rest_chips, pairs[0]))
+    full_up = full_rest[:, :ff_part]
+    full_down = full_rest[:, ff_part:]
 
     grad_mixed = mm("dc,rd->cr", full_out, upstream).astype(low)
     inner = mm("rd,df->rf", normed_two, full_up) + up_bias
@@ -357,6 +374,8 @@
         mixed_part, query_part, pair_all = attend(
             query[span], key_value, grad_mixed[span], positions, places, seq_count, block_len
         )
+        if key_parts:
+            pair_all, key_parts[-1] = lax.optimization_barrier((pair_all, key_parts[-1]))
         pair = lax.psum_scatter(pair_all, "context", scatter_dimension=0, tiled=False)
         mixed.append(mixed_part)
         grad_query_rot.append(query_part)
@@ -388,18 +407,19 @@
     )
     back_one = mm("cr,dc->rd", grad_qkv, full_qkv)
     tilted = over_tensor(back_one * first_gain + back_two * second_gain)
+    grad_late = jnp.concatenate(
+        [grad_out, mm("rd,cr->dc", normed_one, grad_qkv)], axis=1
+    )
+    tilted, quarter_late = lax.optimization_barrier(
+        (tilted, scatter_chips(scatter_core(grad_late)))
+    )
     first_mean = jnp.mean(tilted, axis=-1, keepdims=True)
     second_mean = jnp.mean(tilted * plain, axis=-1, keepdims=True)
     grad_tokens = (
         upstream_wide + inv_std * (tilted - first_mean - plain * second_mean)
     ).reshape(seq_count, block_len, model_width)
 
-    grad_late = jnp.concatenate(
-        [grad_out, mm("rd,cr->dc", normed_one, grad_qkv)], axis=1
-    )
-    quarter_late, own_ff = lax.optimization_barrier(
-        (scatter_chips(scatter_core(grad_late)), own_ff)
-    )
+    quarter_late, own_ff = lax.optimization_barrier((quarter_late, own_ff))
     own_late = lax.psum(quarter_late, "context").astype(f32)
     own_ff = own_ff.astype(f32)
 

time: 484 us -> 453 us (0.936)
  waiting for transfers between devices: 181 us -> 158 us
  blocking collectives: 14.2 us -> 0 us
    all_gather x2 -> x1, waiting for transfers between devices: 28.8 us -> 0.02 us  [body(): key_values.append(lax.all_gather(pair, 'context', axis=0, tiled=False))]
    all_gather x0 -> x1, waiting for transfers between devices: none -> 19.7 us  [body(): key_values = [lax.all_gather(pairs[0], 'context', axis=0, tiled=False)]]
    all_gather x1 -> x0, blocking collectives: 14.2 us -> none  [body(): places = lax.all_gather(positions, 'context', axis=0, tiled=False)]
    psum x1, waiting for transfers between devices: 33.7 us -> 23.8 us  [body(): own_late = lax.psum(quarter_late, 'context').astype(f32)]
    ppermute x2, waiting for transfers between devices: 29.3 us -> 19.6 us  [scatter_chips(): lax.ppermute(send, 'dp', [(i, (i + 2 * step) % count) for i in range(coun...]
    reduce_sum x0 -> x1, other arithmetic: none -> 5.07 us  [body(): jnp.sum(upstream_wide, axis=0)]
    dot_general x2 -> x1, other arithmetic: 7.64 us -> 2.74 us  [mm(): return jnp.einsum(spec, left, right, preferred_element_type=f32)]
    ppermute x11 -> x14, starting transfers between devices: 12.5 us -> 16.9 us  [the longest x10 12.1 us: small_gather(): lax.ppermute(vector, axis, [(i, (i + step) % count) for i in range(count)])]
  transfers between devices with their start and end apart: 23 -> 26, of which waited for: 12 -> 16; matrix products, arithmetic and copies ran while one was open for 22% -> 24% of each run, Pallas kernels for 24% -> 26%
where the time goes in v3:
time: 453 us; the launch traced here: 447 us
  waiting for transfers between devices  158 us (35%)
  Pallas kernels  116 us (26%)
  other arithmetic  55.4 us (12%)
  matrix products  45.7 us (10%)
  local copies, waits for them, and re-layouts  31.9 us (7%)
  starting transfers between devices  24.2 us (5%)
  between operations  15.7 us (3%)
    pallas_call x2, Pallas kernels, attend(): pl.pallas_call(attend_kernel, grid=(seq_count, heads, blocks), in_specs=[...  116 us
    dot_general x12, matrix products, mm(): return jnp.einsum(spec, left, right, preferred_element_type=f32)  45.7 us
    ppermute x2, waiting for transfers between devices, over_tensor(): other = lax.ppermute(low, 'tensor', [(0, 1), (1, 0)])  37.5 us
    ppermute x2, waiting for transfers between devices, gather_chips(): lax.ppermute(shard, 'dp', [(i, (i + 2 * step) % count) for i in range(cou...  32.1 us
    psum x1, waiting for transfers between devices, body(): own_late = lax.psum(quarter_late, 'context').astype(f32)  23.8 us
    all_gather x1, waiting for transfers between devices, body(): key_values = [lax.all_gather(pairs[0], 'context', axis=0, tiled=False)]  19.7 us
    ppermute x2, waiting for transfers between devices, scatter_chips(): lax.ppermute(send, 'dp', [(i, (i + 2 * step) % count) for i in range(coun...  19.6 us
    ppermute x10, starting transfers between devices, small_gather(): lax.ppermute(vector, axis, [(i, (i + step) % count) for i in range(count)])  12.1 us
  transfers between devices with their start and end apart: 26, of which 16 were waited for; matrix products, arithmetic and copies ran while one was open for 24% of the time, Pallas kernels for 26%

profile of v3, /device:TPU:0, one launch (start us, length us, event | category | flops | bytes accessed | tf_op | source)
XLA Modules:
  0.0 446.7 jit_solution(12286248293985849779)
XLA Ops:
  7.2 1.3 fusion.79
  8.6 3.0 collective-permute-start
  11.9 13.0 %collective-permute-done = bf16[192,1536]{1,0:T(8,128)(2,1)S(1)} collective-permute-done((bf16[192,1536]{1,0:T(8,128)(2,1)S(1)}, bf16[192,1536]{1,0:T(8,128)(2,1)S(1)}, u32[]{:S(2)}, u32[]{:S(2)}) %collective-permute-start) | collective-permute-done | bytes 589856 | tf_op jit(solution)/shard_map/ppermute | solution.py:215
  27.7 1.2 pad_maximum_fusion.6
  28.9 1.8 collective-permute-start.2
  30.7 1.4 select_bitcast_fusion.2
  33.1 2.8 fusion.91
  38.1 19.1 %collective-permute-done.2 = bf16[192,3072]{1,0:T(8,128)(2,1)S(1)} collective-permute-done((bf16[192,3072]{1,0:T(8,128)(2,1)S(1)}, bf16[192,3072]{1,0:T(8,128)(2,1)S(1)}, u32[]{:S(2)}, u32[]{:S(2)}) %collective-permute-start.2) | collective-permute-done | bytes 1179680 | tf_op jit(solution)/shard_map/ppermute | solution.py:215
  57.3 1.6 pad_maximum_fusion.2
  59.9 2.7 fusion.82
  62.6 1.6 copy.41
  64.7 2.7 select_bitcast_fusion
  68.6 3.3 multiply_convert_fusion
  71.9 2.9 convolution_convert_fusion
  74.9 6.3 %convert_reduce_fusion = (f32[1536]{0:T(1024)}, bf16[1024,1536]{1,0:T(8,128)(2,1)S(1)}) fusion(f32[1024,1536]{1,0:T(8,128)S(1)} %get-tuple-element.145, f32[1536]{0:T(1024)S(1)} %copy-done.57, bf16[768,3072]{1,0:T(8,128)(2,1)S(1)} %bitcast.217, bf16[1,1024,768]{2,1,0:T(8,128)(2,1)S(1)} %copy-done.31), kind=kOutput, calls=%fused_computation.7 | convolution fusion | flops 2436364800 | bytes 13383680 | tf_op jit(solution)/shard_map/rd,df->rf/dot_general | solution.py:320
  81.1 2.8 convolution_convert_fusion.1
  84.0 1.8 fusion.33
  86.5 3.8 collective-permute-start.8
  91.6 3.4 collective-permute-done.7
  96.5 2.2 slice.241
  99.6 1.3 pad_maximum_fusion.7
  100.9 3.3 fusion.58
  104.3 6.0 %fusion.41 = f32[1024,768]{1,0:T(8,128)} fusion(bf16[1024,1536]{1,0:T(8,128)(2,1)S(1)} %copy-done.60, bf16[768,3072]{1,0:T(8,128)(2,1)} %bitcast.218), kind=kOutput, calls=%fused_computation.83 | convolution fusion | flops 2415919104 | bytes 8650752 | tf_op jit(solution)/shard_map/rf,df->rd/dot_general | solution.py:320
  110.3 19.7 %all-gather.5.cloned.1.call-done = bf16[1536,1024]{1,0:T(8,128)(2,1)} async-done(((bf16[384,1024]{1,0:T(8,128)(2,1)}), bf16[1536,1024]{1,0:T(8,128)(2,1)}) %all-gather.5.cloned.1.call-update) | async-done | bytes 3145744 | tf_op jit(solution)/shard_map/all_gather | solution.py:346
  130.2 7.1 %fusion.45 = f32[1024,768]{1,0:T(8,128)} fusion(bf16[1024,1536]{1,0:T(8,128)(2,1)} %copy-done.58, bf16[768,3072]{1,0:T(8,128)(2,1)} %bitcast.219), kind=kOutput, calls=%fused_computation.87 | convolution fusion | flops 2415919104 | bytes 8650752 | tf_op jit(solution)/shard_map/rf,df->rd/dot_general | solution.py:320
  137.3 4.1 fusion.6
  142.9 57.9 %shard_map.322 = (bf16[192,1024]{1,0:T(8,128)(2,1)S(1)}, f32[192,1024]{1,0:T(8,128)S(1)}, bf16[4,2,192,1024]{3,2,1,0:T(8,128)(2,1)}) custom-call(s32[2,1,512]{2,1,0:T(1,128)S(1)} %bitcast.208, s32[4,1024,128]{2,1,0:T(8,128)S(1)} %broadcast_in_dim.5.key_places, bf16[192,1024]{1,0:T(8,128)(2,1)S(1)} %get-tuple-element.150.query_ref, ...), custom_call_target="tpu_custom_call" | custom-call | flops 38654705664 | bytes 33554432 | tf_op jit(solution)/shard_map/pallas_call | solution.py:166
  202.6 57.8 %shard_map.323 = (bf16[192,1024]{1,0:T(8,128)(2,1)S(1)}, f32[192,1024]{1,0:T(8,128)S(1)}, bf16[4,2,192,1024]{3,2,1,0:T(8,128)(2,1)}) custom-call(s32[2,1,512]{2,1,0:T(1,128)S(1)} %bitcast.209, s32[4,1024,128]{2,1,0:T(8,128)S(1)} %broadcast_in_dim.5.key_places, bf16[192,1024]{1,0:T(8,128)(2,1)S(1)} %copy-done.2, bf16[4,384,1024]{2,1,0:T(8,128)(2,1)} %bitcast.260, ...), custom_call_target="tpu_custom_call" | custom-call | flops 38654705664 | bytes 33554432 | tf_op jit(solution)/shard_map/pallas_call | solution.py:166
  262.1 2.0 slice_bitcast_fusion.1
  264.4 2.5 dynamic-slice_bitcast_fusion
  266.9 1.5 collective-permute-start.5
  268.5 3.5 add_convert_fusion.1
  272.0 1.6 collective-permute-start.9
  273.6 1.7 copy.44
  275.3 19.6 %collective-permute-done.5 = bf16[192,3072]{1,0:T(8,128)(2,1)} collective-permute-done((bf16[192,3072]{1,0:T(8,128)(2,1)}, bf16[192,3072]{1,0:T(8,128)(2,1)}, u32[]{:S(2)}, u32[]{:S(2)}) %collective-permute-start.5) | collective-permute-done | bytes 1179680 | tf_op jit(solution)/shard_map/ppermute | solution.py:258
  294.9 3.0 fusion.40
  299.0 1.2 copy-done.32
  300.2 1.6 fusion.61
  301.8 6.4 %collective-permute-done.9 = bf16[1024,768]{1,0:T(8,128)(2,1)} collective-permute-done((bf16[1024,768]{1,0:T(8,128)(2,1)}, bf16[1024,768]{1,0:T(8,128)(2,1)}, u32[]{:S(2)}, u32[]{:S(2)}) %collective-permute-start.9) | collective-permute-done | bytes 1572896 | tf_op jit(solution)/shard_map/ppermute | solution.py:206
  308.2 3.9 convert_add_fusion.3
  312.1 10.7 %reduce-scatter.5.cloned.1.call-done = bf16[1,2,192,1024]{3,2,1,0:T(8,128)(2,1)} async-done(((bf16[4,2,192,1024]{3,2,1,0:T(8,128)(2,1)}), bf16[1,2,192,1024]{3,2,1,0:T(8,128)(2,1)}) %reduce-scatter.5.cloned.1.call-update) | async-done | bytes 786448 | tf_op jit(solution)/shard_map/reduce_scatter | solution.py:379
  322.8 1.9 slice_bitcast_fusion.2
  326.2 1.3 subtract_convert_fusion.1
  327.5 1.1 pad_maximum_fusion.13
  328.7 2.2 convolution_convert_fusion.2
  333.1 3.9 add_convert_fusion
  337.0 1.5 collective-permute-start.10
  338.6 1.6 fusion.38
  340.3 1.5 collective-permute-start.12
  342.2 31.1 %collective-permute-done.10 = bf16[1024,768]{1,0:T(8,128)(2,1)} collective-permute-done((bf16[1024,768]{1,0:T(8,128)(2,1)}, bf16[1024,768]{1,0:T(8,128)(2,1)}, u32[]{:S(2)}, u32[]{:S(2)}) %collective-permute-start.10) | collective-permute-done | bytes 1572896 | tf_op jit(solution)/shard_map/ppermute | solution.py:206
  373.3 4.0 convert_add_fusion.2
  378.9 4.8 %fusion.84 = (f32[1024]{0:T(1024)S(1)}, f32[1024]{0:T(1024)S(1)}, f32[768]{0:T(1024)S(1)}, f32[768]{0:T(1024)S(1)}, f32[768]{0:T(1024)S(1)}, /*index=5*/f32[768]{0:T(1024)S(1)}) fusion(f32[1024,768]{1,0:T(8,128)} %convert_add_fusion.2, f32[1024]{0:T(1024)S(1)} %copy-done.43, f32[1024]{0:T(1024)S(1)} %copy-done.41, bf16[1,1024,768]{2,1,0:T(8,128)(2,1)S(1)} %copy-done.9, ...), kind=kLoop, calls=%fused_computation.188 | loop fusion | flops 9432064 | bytes 11038720 | tf_op jit(solution)/shard_map/reduce_sum | solution.py:416
  383.8 5.1 %convert_reduce_fusion.2 = (f32[768]{0:T(1024)S(1)}, f32[1,1024,768]{2,1,0:T(8,128)}, bf16[1,1024,768]{2,1,0:T(8,128)(2,1)}) fusion(bf16[1,1024,768]{2,1,0:T(8,128)(2,1)S(1)} %copy-done.33, f32[1024]{0:T(1024)S(1)} %broadcast_multiply_fusion, f32[1024]{0:T(1024)S(1)} %copy-done.41, bf16[1,1024,768]{2,1,0:T(8,128)(2,1)S(1)} %copy-done.9, ...), kind=kLoop, calls=%fused_computation.23 | loop fusion | flops 11009280 | bytes 14181376 | tf_op jit(solution)/shard_map/reduce_sum | solution.py:438
  389.0 1.6 collective-permute-start.14
  390.7 3.0 all-reduce.3.cloned.1.call-done
  393.7 2.3 slice.194
  397.6 2.0 collective-permute-start.18
  400.5 1.1 collective-permute-start.16
  401.7 3.4 collective-permute-done.17
  405.1 1.2 collective-permute-done.16
  407.7 1.5 collective-permute-start.19
  409.2 2.2 collective-permute-done.19
  412.1 23.8 %all-reduce.5.cloned.1.call-done = bf16[192,1536]{1,0:T(8,128)(2,1)} async-done(((bf16[192,1536]{1,0:T(8,128)(2,1)}), bf16[192,1536]{1,0:T(8,128)(2,1)}) %all-reduce.5.cloned.1.call-update) | async-done | bytes 589840 | tf_op jit(solution)/shard_map/psum | solution.py:423
  435.9 1.3 convert_element_type.173
  (221 shorter events, 32.7 us)
Async XLA Ops:
  7.2 4.4 copy-start.8
  7.2 122.7 %all-gather.5.cloned.1.call-start = ((), (), s32[]{:S(2)}) async-start(), calls=%async_computation.6 | async-start | bytes 3932160 | tf_op jit(solution)/shard_map/all_gather | solution.py:346
  8.6 17.6 %copy-start.7 = (s32[1,1024]{1,0:T(1,128)S(1)}, s32[1,1024]{1,0:T(1,128)}, u32[]{:S(2)}) copy-start(s32[1,1024]{1,0:T(1,128)} %param.20) | copy-start | bytes 12292
  8.6 17.6 %copy-start.54 = (f32[384]{0:T(512)S(1)}, f32[384]{0:T(512)}, u32[]{:S(2)}) copy-start(f32[384]{0:T(512)} %param.30) | copy-start | bytes 4612
  8.6 17.6 %copy-start.55 = (f32[384]{0:T(512)S(1)}, f32[384]{0:T(512)}, u32[]{:S(2)}) copy-start(f32[384]{0:T(512)} %param.29) | copy-start | bytes 4612
  8.6 17.6 %copy-start.56 = (f32[384]{0:T(512)S(1)}, f32[384]{0:T(512)}, u32[]{:S(2)}) copy-start(f32[384]{0:T(512)} %param.28) | copy-start | bytes 4612
  8.6 16.3 %collective-permute-start = (bf16[192,1536]{1,0:T(8,128)(2,1)S(1)}, bf16[192,1536]{1,0:T(8,128)(2,1)S(1)}, u32[]{:S(2)}, u32[]{:S(2)}) collective-permute-start(bf16[192,1536]{1,0:T(8,128)(2,1)S(1)} %get-tuple-element.128), channel_id=1, source_target_pairs={{0,16},{8,24},{16,0},{24,8},{1,17},{9,25},{17,1},{25,9},{2,18},{10... | collective-permute-start | bytes 1769480 | tf_op jit(solution)/shard_map/ppermute | solution.py:215
  11.9 15.8 %copy-start.36 = (bf16[1536,192]{0,1:T(8,128)(2,1)S(1)}, bf16[1536,192]{0,1:T(8,128)(2,1)}, u32[]{:S(2)}) copy-start(bf16[1536,192]{0,1:T(8,128)(2,1)} %param.35) | copy-start | bytes 1769476
  11.9 56.5 %copy-start.40 = (f32[1024]{0:T(1024)}, f32[1024]{0:T(1024)S(1)}, u32[]{:S(2)}) copy-start(f32[1024]{0:T(1024)S(1)} %broadcast_multiply_fusion.2) | copy-start | bytes 12292
  26.1 4.6 %collective-permute-start.1 = (bf16[2,192,1536]{2,1,0:T(8,128)(2,1)}, bf16[2,192,1536]{2,1,0:T(8,128)(2,1)}, u32[]{:S(2)}, u32[]{:S(2)}) collective-permute-start(bf16[2,192,1536]{2,1,0:T(8,128)(2,1)} %pad_maximum_fusion.5), channel_id=1, source_target_pairs={{0,8},{8,0},{16,24},{24,16},{1,9},{9,1},{17,25},{25,17},{2,10},{10... | collective-permute-start | bytes 3538952 | tf_op jit(solution)/shard_map/ppermute | solution.py:225
  26.9 41.5 %copy-start.42 = (f32[1024]{0:T(1024)}, f32[1024]{0:T(1024)S(1)}, u32[]{:S(2)}) copy-start(f32[1024]{0:T(1024)S(1)} %add_rsqrt_fusion) | copy-start | bytes 12292
  27.7 8.6 %copy-start.37 = (f32[8,1024]{1,0:T(8,128)}, f32[8,1024]{1,0:T(8,128)S(1)}, u32[]{:S(2)}) copy-start(f32[8,1024]{1,0:T(8,128)S(1)} %get-tuple-element.141) | copy-start | bytes 98308
  28.9 28.4 %collective-permute-start.2 = (bf16[192,3072]{1,0:T(8,128)(2,1)S(1)}, bf16[192,3072]{1,0:T(8,128)(2,1)S(1)}, u32[]{:S(2)}, u32[]{:S(2)}) collective-permute-start(bf16[192,3072]{1,0:T(8,128)(2,1)S(1)} %pad_maximum_fusion.6), channel_id=1, source_target_pairs={{0,16},{8,24},{16,0},{24,8},{1,17},{9,25},{17,1},{25,9},{2,18},{10... | collective-permute-start | bytes 3538952 | tf_op jit(solution)/shard_map/ppermute | solution.py:215
  32.6 3.3 copy-start.17
  59.9 4.9 %collective-permute-start.3 = (bf16[2,192,3072]{2,1,0:T(8,128)(2,1)}, bf16[2,192,3072]{2,1,0:T(8,128)(2,1)}, u32[]{:S(2)}, u32[]{:S(2)}) collective-permute-start(bf16[2,192,3072]{2,1,0:T(8,128)(2,1)} %pad_maximum_fusion.2), channel_id=1, source_target_pairs={{0,8},{8,0},{16,24},{24,16},{1,9},{9,1},{17,25},{25,17},{2,10},{10... | collective-permute-start | bytes 7077896 | tf_op jit(solution)/shard_map/ppermute | solution.py:225
  64.3 137.4 %all-gather.7.cloned.1.call-start = ((), (), s32[]{:S(2)}) async-start(), calls=%async_computation.7 | async-start | bytes 3932160 | tf_op jit(solution)/shard_map/all_gather | solution.py:349
  68.4 6.5 %copy-start.14 = (bf16[2,2,192,3072]{3,2,1,0:T(8,128)(2,1)}, bf16[2,2,192,3072]{3,2,1,0:T(8,128)(2,1)S(1)}, u32[]{:S(2)}) copy-start(bf16[2,2,192,3072]{3,2,1,0:T(8,128)(2,1)S(1)} %pad_maximum_fusion) | copy-start | bytes 14155780
  68.6 3.3 copy-start.31
  71.9 2.9 copy-start.58
  74.8 6.3 %copy-start.26 = (bf16[768,1024]{1,0:T(8,128)(2,1)S(1)}, bf16[768,1024]{1,0:T(8,128)(2,1)}, u32[]{:S(2)}) copy-start(bf16[768,1024]{1,0:T(8,128)(2,1)} %copy.41) | copy-start | bytes 4718596
  81.1 2.8 copy-start.59
  83.9 14.8 %copy-start.29 = (bf16[3,64,1024]{2,1,0:T(8,128)(2,1)S(1)}, bf16[3,64,1024]{2,1,0:T(8,128)(2,1)}, u32[]{:S(2)}) copy-start(bf16[3,64,1024]{2,1,0:T(8,128)(2,1)} %get-tuple-element.122) | copy-start | bytes 1179652
  86.2 51.2 %collective-permute-start.4 = (bf16[2,192,3072]{2,1,0:T(8,128)(2,1)}, bf16[2,192,3072]{2,1,0:T(8,128)(2,1)}, u32[]{:S(2)}, u32[]{:S(2)}) collective-permute-start(bf16[2,192,3072]{2,1,0:T(8,128)(2,1)} %fusion.33), channel_id=1, source_target_pairs={{0,8},{8,0},{16,24},{24,16},{1,9},{9,1},{17,25},{25,17},{2,10},{10... | collective-permute-start | bytes 7077896 | tf_op jit(solution)/shard_map/ppermute | solution.py:247
  86.5 5.1 %collective-permute-start.8 = (s32[1,1024]{1,0:T(1,128)S(1)}, s32[1,1024]{1,0:T(1,128)S(1)}, u32[]{:S(2)}, u32[]{:S(2)}) collective-permute-start(s32[1,1024]{1,0:T(1,128)S(1)} %copy-done.7), channel_id=1, source_target_pairs={{0,6},{2,0},{4,2},{6,4},{1,7},{3,1},{5,3},{7,5},{8,14},{10,8},{12,... | collective-permute-start | bytes 12296 | tf_op jit(solution)/shard_map/ppermute | solution.py:271
  90.3 4.7 %collective-permute-start.7 = (s32[1,1024]{1,0:T(1,128)S(1)}, s32[1,1024]{1,0:T(1,128)S(1)}, u32[]{:S(2)}, u32[]{:S(2)}) collective-permute-start(s32[1,1024]{1,0:T(1,128)S(1)} %copy-done.7), channel_id=1, source_target_pairs={{0,4},{2,6},{4,0},{6,2},{1,5},{3,7},{5,1},{7,3},{8,12},{10,14},{12... | collective-permute-start | bytes 12296 | tf_op jit(solution)/shard_map/ppermute | solution.py:271
  90.3 5.6 %collective-permute-start.6 = (s32[1,1024]{1,0:T(1,128)S(1)}, s32[1,1024]{1,0:T(1,128)S(1)}, u32[]{:S(2)}, u32[]{:S(2)}) collective-permute-start(s32[1,1024]{1,0:T(1,128)S(1)} %copy-done.7), channel_id=1, source_target_pairs={{0,2},{2,4},{4,6},{6,0},{1,3},{3,5},{5,7},{7,1},{8,10},{10,12},{12... | collective-permute-start | bytes 12296 | tf_op jit(solution)/shard_map/ppermute | solution.py:271
  99.6 4.7 %copy-start.60 = (bf16[1024,1536]{1,0:T(8,128)(2,1)S(1)}, bf16[1024,1536]{1,0:T(8,128)(2,1)}, u32[]{:S(2)}) copy-start(bf16[1024,1536]{1,0:T(8,128)(2,1)} %copy-done.59) | copy-start | bytes 9437188
  129.9 132.2 %reduce-scatter.3.cloned.1.call-start = ((), (), s32[]{:S(2)}) async-start(), calls=%async_computation.2 | async-start | bytes 3932160 | tf_op jit(solution)/shard_map/reduce_scatter | solution.py:379
  130.2 7.1 %copy-start.11 = (bf16[2,2,192,1536]{3,2,1,0:T(8,128)(2,1)S(1)}, bf16[2,2,192,1536]{3,2,1,0:T(8,128)(2,1)}, u32[]{:S(2)}) copy-start(bf16[2,2,192,1536]{3,2,1,0:T(8,128)(2,1)} %copy-done.10) | copy-start | bytes 7077892
  137.3 4.1 copy-start.34
  201.6 121.2 %reduce-scatter.5.cloned.1.call-start = ((), (), s32[]{:S(2)}) async-start(), calls=%async_computation.3 | async-start | bytes 3932160 | tf_op jit(solution)/shard_map/reduce_scatter | solution.py:379
  264.1 4.4 copy-start.4
  264.1 4.4 copy-start.6
  264.1 129.6 %all-reduce.3.cloned.1.call-start = ((), (), s32[]{:S(2)}) async-start(), calls=%async_computation.4 | async-start | bytes 2359296 | tf_op jit(solution)/shard_map/psum | solution.py:393
  264.4 4.1 copy-start.20
  266.9 28.0 %collective-permute-start.5 = (bf16[192,3072]{1,0:T(8,128)(2,1)}, bf16[192,3072]{1,0:T(8,128)(2,1)}, u32[]{:S(2)}, u32[]{:S(2)}) collective-permute-start(bf16[192,3072]{1,0:T(8,128)(2,1)} %dynamic-slice_bitcast_fusion), channel_id=1, source_target_pairs={{0,16},{8,24},{16,0},{24,8},{1,17},{9,25},{17,1},{25,9},{2,18},{10... | collective-permute-start | bytes 3538952 | tf_op jit(solution)/shard_map/ppermute | solution.py:258
  268.5 5.1 %copy-start.12 = (bf16[768,1024]{0,1:T(8,128)(2,1)S(1)}, bf16[768,1024]{0,1:T(8,128)(2,1)}, u32[]{:S(2)}) copy-start(bf16[768,1024]{0,1:T(8,128)(2,1)} %get-tuple-element.109) | copy-start | bytes 4718596
  272.0 36.2 %collective-permute-start.9 = (bf16[1024,768]{1,0:T(8,128)(2,1)}, bf16[1024,768]{1,0:T(8,128)(2,1)}, u32[]{:S(2)}, u32[]{:S(2)}) collective-permute-start(bf16[1024,768]{1,0:T(8,128)(2,1)} %add_convert_fusion.1), channel_id=1, source_target_pairs={{0,1},{1,0},{2,3},{3,2},{4,5},{5,4},{6,7},{7,6},{8,9},{9,8},{10,11... | collective-permute-start | bytes 4718600 | tf_op jit(solution)/shard_map/ppermute | solution.py:206
  275.3 22.7 %copy-start.1 = (f32[192,1024]{1,0:T(8,128)S(1)}, f32[192,1024]{1,0:T(8,128)}, u32[]{:S(2)}) copy-start(f32[192,1024]{1,0:T(8,128)} %copy-done) | copy-start | bytes 2359300
  298.1 3.7 copy-start.15
  301.8 22.9 %copy-start.30 = (bf16[192,1024]{1,0:T(8,128)(2,1)S(1)}, bf16[192,1024]{1,0:T(8,128)(2,1)}, u32[]{:S(2)}) copy-start(bf16[192,1024]{1,0:T(8,128)(2,1)} %get-tuple-element.62) | copy-start | bytes 1179652
  326.2 2.5 copy-start.25
  328.7 3.4 copy-start.21
  328.7 3.4 copy-start.23
  332.1 6.5 %collective-permute-start.11 = (bf16[2,192,1536]{2,1,0:T(8,128)(2,1)}, bf16[2,192,1536]{2,1,0:T(8,128)(2,1)}, u32[]{:S(2)}, u32[]{:S(2)}) collective-permute-start(bf16[2,192,1536]{2,1,0:T(8,128)(2,1)} %fusion.65), channel_id=1, source_target_pairs={{0,8},{8,0},{16,24},{24,16},{1,9},{9,1},{17,25},{25,17},{2,10},{10... | collective-permute-start | bytes 3538952 | tf_op jit(solution)/shard_map/ppermute | solution.py:247
  337.0 36.3 %collective-permute-start.10 = (bf16[1024,768]{1,0:T(8,128)(2,1)}, bf16[1024,768]{1,0:T(8,128)(2,1)}, u32[]{:S(2)}, u32[]{:S(2)}) collective-permute-start(bf16[1024,768]{1,0:T(8,128)(2,1)} %get-tuple-element.146), channel_id=1, source_target_pairs={{0,1},{1,0},{2,3},{3,2},{4,5},{5,4},{6,7},{7,6},{8,9},{9,8},{10,11... | collective-permute-start | bytes 4718600 | tf_op jit(solution)/shard_map/ppermute | solution.py:206
  338.5 97.4 %all-reduce.5.cloned.1.call-start = ((), (), s32[]{:S(2)}) async-start(), calls=%async_computation.5 | async-start | bytes 1179648 | tf_op jit(solution)/shard_map/psum | solution.py:423
  338.6 3.3 copy-start.22
  338.6 3.2 copy-start.28
  340.3 37.0 %collective-permute-start.12 = (bf16[192,1536]{1,0:T(8,128)(2,1)S(1)}, bf16[192,1536]{1,0:T(8,128)(2,1)S(1)}, u32[]{:S(2)}, u32[]{:S(2)}) collective-permute-start(bf16[192,1536]{1,0:T(8,128)(2,1)S(1)} %dynamic-slice_bitcast_fusion.1), channel_id=1, source_target_pairs={{0,16},{8,24},{16,0},{24,8},{1,17},{9,25},{17,1},{25,9},{2,18},{10... | collective-permute-start | bytes 1769480 | tf_op jit(solution)/shard_map/ppermute | solution.py:258
  342.2 36.0 %copy-start.41 = (f32[1024]{0:T(1024)S(1)}, f32[1024]{0:T(1024)}, u32[]{:S(2)}) copy-start(f32[1024]{0:T(1024)} %copy-done.40) | copy-start | bytes 12292
  342.2 36.0 %copy-start.43 = (f32[1024]{0:T(1024)S(1)}, f32[1024]{0:T(1024)}, u32[]{:S(2)}) copy-start(f32[1024]{0:T(1024)} %copy-done.42) | copy-start | bytes 12292
  378.9 4.9 %copy-start.33 = (bf16[1,1024,768]{2,1,0:T(8,128)(2,1)S(1)}, bf16[1,1024,768]{2,1,0:T(8,128)(2,1)}, u32[]{:S(2)}) copy-start(bf16[1,1024,768]{2,1,0:T(8,128)(2,1)} %param.37) | copy-start | bytes 4718596
  378.9 4.9 %copy-start.52 = (f32[768]{0:T(1024)S(1)}, f32[768]{0:T(1024)}, u32[]{:S(2)}) copy-start(f32[768]{0:T(1024)} %param.36) | copy-start | bytes 9220
  378.9 4.9 %copy-start.53 = (f32[768]{0:T(1024)S(1)}, f32[768]{0:T(1024)}, u32[]{:S(2)}) copy-start(f32[768]{0:T(1024)} %param.32) | copy-start | bytes 9220
  383.8 5.1 %copy-start.46 = (f32[1536]{0:T(1024)S(1)}, f32[1536]{0:T(1024)}, u32[]{:S(2)}) copy-start(f32[1536]{0:T(1024)} %get-tuple-element.148) | copy-start | bytes 18436
  388.9 8.5 %collective-permute-start.15 = (f32[1,6528]{1,0:T(1,128)S(1)}, f32[1,6528]{1,0:T(1,128)S(1)}, u32[]{:S(2)}, u32[]{:S(2)}) collective-permute-start(f32[1,6528]{1,0:T(1,128)S(1)} %reshape.332), channel_id=1, source_target_pairs={{0,24},{8,0},{16,8},{24,16},{1,25},{9,1},{17,9},{25,17},{2,26},{10... | collective-permute-start | bytes 78344 | tf_op jit(solution)/shard_map/ppermute | solution.py:271
  389.0 8.5 %collective-permute-start.14 = (f32[1,6528]{1,0:T(1,128)S(1)}, f32[1,6528]{1,0:T(1,128)S(1)}, u32[]{:S(2)}, u32[]{:S(2)}) collective-permute-start(f32[1,6528]{1,0:T(1,128)S(1)} %reshape.332), channel_id=1, source_target_pairs={{0,16},{8,24},{16,0},{24,8},{1,17},{9,25},{17,1},{25,9},{2,18},{10... | collective-permute-start | bytes 78344 | tf_op jit(solution)/shard_map/ppermute | solution.py:271
  390.5 6.9 %collective-permute-start.13 = (f32[1,6528]{1,0:T(1,128)S(1)}, f32[1,6528]{1,0:T(1,128)S(1)}, u32[]{:S(2)}, u32[]{:S(2)}) collective-permute-start(f32[1,6528]{1,0:T(1,128)S(1)} %reshape.332), channel_id=1, source_target_pairs={{0,8},{8,16},{16,24},{24,0},{1,9},{9,17},{17,25},{25,1},{2,10},{10... | collective-permute-start | bytes 78344 | tf_op jit(solution)/shard_map/ppermute | solution.py:271
  397.6 4.1 collective-permute-start.18
  399.6 5.5 %collective-permute-start.17 = (f32[1,6528]{1,0:T(1,128)S(1)}, f32[1,6528]{1,0:T(1,128)S(1)}, u32[]{:S(2)}, u32[]{:S(2)}) collective-permute-start(f32[1,6528]{1,0:T(1,128)S(1)} %fusion.99), channel_id=1, source_target_pairs={{0,4},{2,6},{4,0},{6,2},{1,5},{3,7},{5,1},{7,3},{8,12},{10,14},{12... | collective-permute-start | bytes 78344 | tf_op jit(solution)/shard_map/ppermute | solution.py:271
  400.5 5.8 %collective-permute-start.16 = (f32[1,6528]{1,0:T(1,128)S(1)}, f32[1,6528]{1,0:T(1,128)S(1)}, u32[]{:S(2)}, u32[]{:S(2)}) collective-permute-start(f32[1,6528]{1,0:T(1,128)S(1)} %fusion.99), channel_id=1, source_target_pairs={{0,2},{2,4},{4,6},{6,0},{1,3},{3,5},{5,7},{7,1},{8,10},{10,12},{12... | collective-permute-start | bytes 78344 | tf_op jit(solution)/shard_map/ppermute | solution.py:271
  407.7 3.7 collective-permute-start.19
  409.2 30.2 %copy-start.45 = (f32[768]{0:T(1024)}, f32[768]{0:T(1024)S(1)}, u32[]{:S(2)}) copy-start(f32[768]{0:T(1024)S(1)} %slice_reduce_fusion.1) | copy-start | bytes 9220
  (23 other events, 32.5 us)
Sparse Core Ops, SparseCore 0:
  64.4 65.4 all-gather.4
  132.1 61.9 all-gather.6
  201.7 58.5 reduce-scatter.2
  264.2 58.5 reduce-scatter.4
  338.6 54.9 all-reduce.2
  396.4 39.4 all-reduce.4
